TPU v7x, 32 devices: a whole 2x2x4 slice. The times are simulated.
32 devices in a mesh: slab: 4 (over x, core), mapx: 4 (over z), mapy: 2 (over y).
Axes of the slice: x: 2, y: 2, z: 4, core: 2. Of those that a mesh axis runs over, the one named last changes fastest.
Arguments:
- pressure: float32 [32, 384, 512], P('slab', 'mapx', 'mapy'), may hold values from -2 to 2
- porosity: float32 [32, 384, 512], P('slab', 'mapx', 'mapy'), may hold values from 0.1 to 0.5
- lithology: int32 [32, 384, 512], P('slab', 'mapx', 'mapy'), may hold values from 0 to 3
- layer_solid: float32 [32], P('slab'), may hold values from 0.05 to 0.15
Outputs:
- pressure_new: float32 [32, 384, 512], P('slab', 'mapx', 'mapy')
- porosity_new: float32 [32, 384, 512], P('slab', 'mapx', 'mapy')
- thickness_new: float32 [32, 384, 512], P('slab', 'mapx', 'mapy')
All inputs are finite; a program needn't handle non-finite values.
Results may differ from a plain program's by a relative error of at most 0.00015.
Values sent between devices are 32-bit elements; how exact they have to be, the bound alone decides.
A program may use at most 64 MiB of HBM per device.

v0:
```python
import jax
import jax.numpy as jnp
from jax import lax
from jax.sharding import PartitionSpec as P

PHI_SURFACE = (0.45, 0.55, 0.65, 0.4)
ATHY_RATE = (0.25, 0.45, 0.8, 0.35)
MOB_BASE = (1.0, 0.0, -1.5, -0.5)
MOB_SLOPE = (6.0, 5.0, 8.0, 4.0)
GRAIN_DENSITY = (2.65, 2.68, 2.72, 2.71)
WATER_DENSITY = 1.03
SPECTRUM_MID = 1.0
SPECTRUM_HALF = 0.95
SIGMA_RATIO = SPECTRUM_MID / SPECTRUM_HALF
RHO_FIRST = 1.0 / SIGMA_RATIO
RHO_SECOND = 1.0 / (2.0 * SIGMA_RATIO - RHO_FIRST)


def padded_2(array, sides, width):
    for axis, dim in sides:
        size, length = (lax.axis_size(axis), array.shape[dim])
        up = [(i, (i + 1) % size) for i in range(size - 1)]
        down = [(j, i) for i, j in up]
        last = lax.slice_in_dim(array, length - width, length, axis=dim)
        leading = lax.slice_in_dim(array, 0, width, axis=dim)
        before = lax.ppermute(last, axis, up)
        after = lax.ppermute(leading, axis, down)
        array = jnp.concatenate([before, array, after], axis=dim)
    return array


def carried_in(value, axis, join, neutral):
    count, mine = (lax.axis_size(axis), lax.axis_index(axis))
    pieces = lax.all_gather(value, axis)
    total = jnp.full_like(value, 0) + jnp.asarray(neutral, value.dtype)

    def hop(position, total):
        longer = join(total, pieces[position])
        return jnp.where(position < mine, longer, total)

    return lax.fori_loop(0, count - 1, hop, total)


def lookup(lithology, table):
    result = jnp.zeros(lithology.shape, jnp.float32)
    for index, entry in enumerate(table):
        result = result + jnp.where(lithology == index, jnp.float32(entry), jnp.float32(0.0))
    return result


def neighbours(padded):
    return [
        padded[2:, 1:-1, 1:-1],
        padded[:-2, 1:-1, 1:-1],
        padded[1:-1, 2:, 1:-1],
        padded[1:-1, :-2, 1:-1],
        padded[1:-1, 1:-1, 2:],
        padded[1:-1, 1:-1, :-2],
    ]


def harmonic(centre, padded):
    result = []
    for other in neighbours(padded):
        total = centre + other
        safe_total = jnp.where(total > 0.0, total, 1.0)
        result.append(2.0 * centre * other / safe_total)
    return result


def operate_padded(trans, field, padded):
    result = field
    for weight, beside in zip(trans, neighbours(padded)):
        result = result + weight * (field - beside)
    return result


def add_loads(earlier, later):
    return earlier + later


def body(pressure, porosity, lithology, layer_solid):
    mobility = jnp.exp(
        lookup(lithology, MOB_BASE) + lookup(lithology, MOB_SLOPE) * (porosity - 0.35)
    )
    mob_padded = padded_2(mobility, (("slab", 0), ("mapx", 1), ("mapy", 2)), 1)
    trans = harmonic(mobility, mob_padded)
    diag = 1.0 + trans[0] + trans[1] + trans[2] + trans[3] + trans[4] + trans[5]

    def operate(field):
        padded = padded_2(field, (("slab", 0), ("mapx", 1), ("mapy", 2)), 1)
        return operate_padded(trans, field, padded)

    first_res = pressure - operate(pressure)
    first_step = first_res / (SPECTRUM_MID * diag)
    middle = pressure + first_step
    second_res = pressure - operate(middle)
    second_step = (
        RHO_SECOND * RHO_FIRST * first_step + 2.0 * RHO_SECOND / SPECTRUM_HALF * second_res / diag
    )
    pressure_new = middle + second_step
    solid = layer_solid[:, None, None]
    load = (lookup(lithology, GRAIN_DENSITY) + WATER_DENSITY * porosity / (1.0 - porosity)) * solid
    local_sum = jnp.cumsum(load, axis=0)
    column_total = local_sum[-1]
    above = carried_in(column_total, "slab", add_loads, jnp.zeros_like(column_total))
    overburden = above[None] + local_sum - 0.5 * load
    stress = jnp.maximum(overburden - pressure_new, 0.0)
    porosity_new = lookup(lithology, PHI_SURFACE) * jnp.exp(-lookup(lithology, ATHY_RATE) * stress)
    thickness_new = solid / (1.0 - porosity_new)
    return (pressure_new, porosity_new, thickness_new)


def solution(mesh):
    in_specs = (
        P("slab", "mapx", "mapy"),
        P("slab", "mapx", "mapy"),
        P("slab", "mapx", "mapy"),
        P("slab"),
    )
    out_specs = (P("slab", "mapx", "mapy"), P("slab", "mapx", "mapy"), P("slab", "mapx", "mapy"))
    return jax.shard_map(body, mesh=mesh, in_specs=in_specs, out_specs=out_specs, check_vma=False)
```

profile of v0, /device:TPU:0, one launch (start us, length us, event | category | flops | bytes accessed | tf_op | source)
XLA Modules:
  0.0 103.5 jit_solution(13851642171913817331)
XLA Ops:
  1.6 1.3 %collective-permute-start.1 = (f32[1,96,256]{2,1,0:T(8,128)S(1)}, f32[1,96,256]{2,1,0:T(8,128)S(1)}, u32[]{:S(2)}, u32[]{:S(2)}) collective-permute-start(f32[1,96,256]{2,1,0:T(8,128)S(1)} %get-tuple-element.135), channel_id=1, source_target_pairs={{8,0},{16,8},{24,16},{9,1},{17,9},{25,17},{10,2},{18,10},{26,18},{... | collective-permute-start | bytes 294920 | tf_op jit(solution)/shard_map/ppermute | solution.py:27
  2.9 3.0 %collective-permute-start.3 = (f32[1,96,256]{2,1,0:T(8,128)S(1)}, f32[1,96,256]{2,1,0:T(8,128)S(1)}, u32[]{:S(2)}, u32[]{:S(2)}) collective-permute-start(f32[1,96,256]{2,1,0:T(8,128)S(1)} %get-tuple-element.136), channel_id=1, source_target_pairs={{0,8},{8,16},{16,24},{1,9},{9,17},{17,25},{2,10},{10,18},{18,26},{... | collective-permute-start | bytes 294920 | tf_op jit(solution)/shard_map/ppermute | solution.py:26
  5.9 3.1 %add_exponential_fusion = (f32[8,96,256]{2,1,0:T(8,128)S(1)}, pred[8,96,256]{2,1,0:T(8,128)(4,1)S(1)}, pred[8,96,256]{2,1,0:T(8,128)(4,1)}, pred[8,96,256]{2,1,0:T(8,128)(4,1)}, pred[8,96,256]{2,1,0:T(8,128)(4,1)}) fusion(f32[8,96,256]{2,1,0:T(8,128)} %param.7, s32[8,96,256]{2,1,0:T(8,128)} %param.8), kind=kLoop, calls=%fused_computation.113 | loop fusion | flops 3735552 | bytes 3145728 | tf_op jit(solution)/shard_map/exp | solution.py:83
  9.0 4.5 %collective-permute-start.2 = (f32[1,96,256]{2,1,0:T(8,128)S(1)}, f32[1,96,256]{2,1,0:T(8,128)S(1)}, u32[]{:S(2)}, u32[]{:S(2)}) collective-permute-start(f32[1,96,256]{2,1,0:T(8,128)S(1)} %get-tuple-element.133), channel_id=1, source_target_pairs={{0,8},{8,16},{16,24},{1,9},{9,17},{17,25},{2,10},{10,18},{18,26},{... | collective-permute-start | bytes 294920 | tf_op jit(solution)/shard_map/ppermute | solution.py:26
  13.5 1.3 %collective-permute-start = (f32[1,96,256]{2,1,0:T(8,128)S(1)}, f32[1,96,256]{2,1,0:T(8,128)S(1)}, u32[]{:S(2)}, u32[]{:S(2)}) collective-permute-start(f32[1,96,256]{2,1,0:T(8,128)S(1)} %get-tuple-element.134), channel_id=1, source_target_pairs={{8,0},{16,8},{24,16},{9,1},{17,9},{25,17},{10,2},{18,10},{26,18},{... | collective-permute-start | bytes 294920 | tf_op jit(solution)/shard_map/ppermute | solution.py:27
  15.0 1.3 %collective-permute-start.5 = (f32[10,1,256]{2,0,1:T(8,128)S(1)}, f32[10,1,256]{2,0,1:T(8,128)S(1)}, u32[]{:S(2)}, u32[]{:S(2)}) collective-permute-start(f32[10,1,256]{2,0,1:T(8,128)S(1)} %copy.65), channel_id=1, source_target_pairs={{2,0},{4,2},{6,4},{3,1},{5,3},{7,5},{10,8},{12,10},{14,12},{11,9},... | collective-permute-start | bytes 30728 | tf_op jit(solution)/shard_map/ppermute | solution.py:27
  16.3 4.5 %collective-permute-start.7 = (f32[10,1,256]{2,0,1:T(8,128)S(1)}, f32[10,1,256]{2,0,1:T(8,128)S(1)}, u32[]{:S(2)}, u32[]{:S(2)}) collective-permute-start(f32[10,1,256]{2,0,1:T(8,128)S(1)} %copy.67), channel_id=1, source_target_pairs={{0,2},{2,4},{4,6},{1,3},{3,5},{5,7},{8,10},{10,12},{12,14},{9,11},... | collective-permute-start | bytes 30728 | tf_op jit(solution)/shard_map/ppermute | solution.py:26
  20.9 1.3 %collective-permute-start.4 = (f32[10,1,256]{2,0,1:T(8,128)S(1)}, f32[10,1,256]{2,0,1:T(8,128)S(1)}, u32[]{:S(2)}, u32[]{:S(2)}) collective-permute-start(f32[10,1,256]{2,0,1:T(8,128)S(1)} %copy.64), channel_id=1, source_target_pairs={{2,0},{4,2},{6,4},{3,1},{5,3},{7,5},{10,8},{12,10},{14,12},{11,9},... | collective-permute-start | bytes 30728 | tf_op jit(solution)/shard_map/ppermute | solution.py:27
  22.2 4.5 %collective-permute-start.6 = (f32[10,1,256]{2,0,1:T(8,128)S(1)}, f32[10,1,256]{2,0,1:T(8,128)S(1)}, u32[]{:S(2)}, u32[]{:S(2)}) collective-permute-start(f32[10,1,256]{2,0,1:T(8,128)S(1)} %copy.66), channel_id=1, source_target_pairs={{0,2},{2,4},{4,6},{1,3},{3,5},{5,7},{8,10},{10,12},{12,14},{9,11},... | collective-permute-start | bytes 30728 | tf_op jit(solution)/shard_map/ppermute | solution.py:26
  28.1 3.4 %collective-permute-start.11 = (f32[10,98,1]{1,0,2:T(8,128)S(1)}, f32[10,98,1]{1,0,2:T(8,128)S(1)}, u32[]{:S(2)}, u32[]{:S(2)}) collective-permute-start(f32[10,98,1]{1,0,2:T(8,128)S(1)} %copy.52), channel_id=1, source_target_pairs={{0,1},{2,3},{4,5},{6,7},{8,9},{10,11},{12,13},{14,15},{16,17},{18,... | collective-permute-start | bytes 11768 | tf_op jit(solution)/shard_map/ppermute | solution.py:26
  31.5 1.3 %collective-permute-start.9 = (f32[10,98,1]{1,0,2:T(8,128)S(1)}, f32[10,98,1]{1,0,2:T(8,128)S(1)}, u32[]{:S(2)}, u32[]{:S(2)}) collective-permute-start(f32[10,98,1]{1,0,2:T(8,128)S(1)} %copy.48), channel_id=1, source_target_pairs={{1,0},{3,2},{5,4},{7,6},{9,8},{11,10},{13,12},{15,14},{17,16},{19,... | collective-permute-start | bytes 11768 | tf_op jit(solution)/shard_map/ppermute | solution.py:27
  33.8 1.3 %collective-permute-start.8 = (f32[10,98,1]{1,0,2:T(8,128)S(1)}, f32[10,98,1]{1,0,2:T(8,128)S(1)}, u32[]{:S(2)}, u32[]{:S(2)}) collective-permute-start(f32[10,98,1]{1,0,2:T(8,128)S(1)} %copy.44), channel_id=1, source_target_pairs={{1,0},{3,2},{5,4},{7,6},{9,8},{11,10},{13,12},{15,14},{17,16},{19,... | collective-permute-start | bytes 11768 | tf_op jit(solution)/shard_map/ppermute | solution.py:27
  35.4 4.5 %collective-permute-start.10 = (f32[10,98,1]{1,0,2:T(8,128)S(1)}, f32[10,98,1]{1,0,2:T(8,128)S(1)}, u32[]{:S(2)}, u32[]{:S(2)}) collective-permute-start(f32[10,98,1]{1,0,2:T(8,128)S(1)} %copy.50), channel_id=1, source_target_pairs={{0,1},{2,3},{4,5},{6,7},{8,9},{10,11},{12,13},{14,15},{16,17},{18,... | collective-permute-start | bytes 11768 | tf_op jit(solution)/shard_map/ppermute | solution.py:26
  43.1 1.1 %copy.51 = f32[10,98,1]{2,1,0:T(8,128)} copy(f32[10,98,1]{1,0,2:T(8,128)S(1)} %collective-permute-done.10) | data formatting | bytes 7840 | tf_op jit(solution)/shard_map/ppermute | solution.py:26
  44.2 7.5 %fusion.55 = (f32[8,96,256]{2,1,0:T(8,128)S(1)}, f32[8,96,256]{2,1,0:T(8,128)}) fusion(f32[8,96,256]{2,1,0:T(8,128)S(1)} %copy-done, f32[10,1,256]{2,1,0:T(1,128)} %copy-done.13, f32[10,96,256]{2,1,0:T(8,128)} %copy-done.2, f32[10,1,256]{2,1,0:T(1,128)} %copy-done.14, f32[10,98,1]{2,1,0:T(8,128)} %copy.53, f32[8,96,256]{2,1,0:T(8,128)S(1)} %get-tuple-element.114, ...), kind=kLoop, calls=%fused_computation.128 | loop fusion | flops 16908288 | bytes 4578624 | tf_op jit(solution)/shard_map/add | solution.py:96
  51.7 1.3 %collective-permute-start.13 = (f32[1,96,256]{2,1,0:T(8,128)S(1)}, f32[1,96,256]{2,1,0:T(8,128)S(1)}, u32[]{:S(2)}, u32[]{:S(2)}) collective-permute-start(f32[1,96,256]{2,1,0:T(8,128)S(1)} %get-tuple-element.131), channel_id=1, source_target_pairs={{0,8},{8,16},{16,24},{1,9},{9,17},{17,25},{2,10},{10,18},{18,26},{... | collective-permute-start | bytes 294920 | tf_op jit(solution)/shard_map/ppermute | solution.py:26
  53.0 1.3 %collective-permute-start.12 = (f32[1,96,256]{2,1,0:T(8,128)S(1)}, f32[1,96,256]{2,1,0:T(8,128)S(1)}, u32[]{:S(2)}, u32[]{:S(2)}) collective-permute-start(f32[1,96,256]{2,1,0:T(8,128)S(1)} %get-tuple-element.132), channel_id=1, source_target_pairs={{8,0},{16,8},{24,16},{9,1},{17,9},{25,17},{10,2},{18,10},{26,18},{... | collective-permute-start | bytes 294920 | tf_op jit(solution)/shard_map/ppermute | solution.py:27
  55.9 3.3 %collective-permute-done.12 = f32[1,96,256]{2,1,0:T(8,128)S(1)} collective-permute-done((f32[1,96,256]{2,1,0:T(8,128)S(1)}, f32[1,96,256]{2,1,0:T(8,128)S(1)}, u32[]{:S(2)}, u32[]{:S(2)}) %collective-permute-start.12) | collective-permute-done | bytes 98336 | tf_op jit(solution)/shard_map/ppermute | solution.py:27
  60.5 1.3 %collective-permute-start.14 = (f32[10,1,256]{2,0,1:T(8,128)}, f32[10,1,256]{2,0,1:T(8,128)}, u32[]{:S(2)}, u32[]{:S(2)}) collective-permute-start(f32[10,1,256]{2,0,1:T(8,128)} %copy.68), channel_id=1, source_target_pairs={{2,0},{4,2},{6,4},{3,1},{5,3},{7,5},{10,8},{12,10},{14,12},{11,9},... | collective-permute-start | bytes 30728 | tf_op jit(solution)/shard_map/ppermute | solution.py:27
  61.8 5.1 %collective-permute-start.15 = (f32[10,1,256]{2,0,1:T(8,128)}, f32[10,1,256]{2,0,1:T(8,128)}, u32[]{:S(2)}, u32[]{:S(2)}) collective-permute-start(f32[10,1,256]{2,0,1:T(8,128)} %copy.69), channel_id=1, source_target_pairs={{0,2},{2,4},{4,6},{1,3},{3,5},{5,7},{8,10},{10,12},{12,14},{9,11},... | collective-permute-start | bytes 30728 | tf_op jit(solution)/shard_map/ppermute | solution.py:26
  66.9 8.3 %all_gather.3 = f32[4,96,256]{2,1,0:T(8,128)} all-gather(f32[1,96,256]{2,1,0:T(8,128)S(1)} %slice.178), channel_id=1, replica_groups=mesh['slab'=4,'mapx'=4,'mapy'=2] {'slab'}, dimensions={0}, use_global_device_ids=true | all-gather | bytes 491520 | tf_op jit(solution)/shard_map/all_gather | solution.py:34
  76.7 1.1 %pad_maximum_fusion.2 = f32[10,98,256]{2,1,0:T(8,128)S(1)} fusion(f32[10,1,256]{2,1,0:T(1,128)S(1)} %copy.55, f32[1,96,256]{2,1,0:T(8,128)} %copy-done.9, f32[8,96,256]{2,1,0:T(8,128)S(1)} %get-tuple-element.112, f32[1,96,256]{2,1,0:T(8,128)} %copy-done.8, f32[10,1,256]{2,1,0:T(1,128)S(1)} %copy.57), kind=kLoop, calls=%fused_computation.9 | loop fusion | flops 1003520 | bytes 2007040 | tf_op jit(solution)/shard_map/concatenate | solution.py:28
  77.8 1.1 %fusion.57 = (f32[10,98,1]{2,1,0:T(8,128)}, f32[10,98,1]{2,1,0:T(8,128)}) fusion(f32[10,98,256]{2,1,0:T(8,128)S(1)} %pad_maximum_fusion.2), kind=kLoop, calls=%fused_computation.129 | loop fusion | bytes 15680 | tf_op jit(solution)/shard_map/slice | solution.py:25
  78.9 1.9 %copy.60 = f32[10,98,1]{1,0,2:T(8,128)} copy(f32[10,98,1]{2,1,0:T(8,128)} %get-tuple-element.119) | data formatting | bytes 7840 | tf_op jit(solution)/shard_map/slice | solution.py:25
  80.9 1.9 %copy.62 = f32[10,98,1]{1,0,2:T(8,128)} copy(f32[10,98,1]{2,1,0:T(8,128)} %get-tuple-element.120) | data formatting | bytes 7840 | tf_op jit(solution)/shard_map/slice | solution.py:24
  82.8 2.9 %collective-permute-start.17 = (f32[10,98,1]{1,0,2:T(8,128)}, f32[10,98,1]{1,0,2:T(8,128)}, u32[]{:S(2)}, u32[]{:S(2)}) collective-permute-start(f32[10,98,1]{1,0,2:T(8,128)} %copy.62), channel_id=1, source_target_pairs={{0,1},{2,3},{4,5},{6,7},{8,9},{10,11},{12,13},{14,15},{16,17},{18,... | collective-permute-start | bytes 11768 | tf_op jit(solution)/shard_map/ppermute | solution.py:26
  85.7 1.3 %collective-permute-start.16 = (f32[10,98,1]{1,0,2:T(8,128)}, f32[10,98,1]{1,0,2:T(8,128)}, u32[]{:S(2)}, u32[]{:S(2)}) collective-permute-start(f32[10,98,1]{1,0,2:T(8,128)} %copy.60), channel_id=1, source_target_pairs={{1,0},{3,2},{5,4},{7,6},{9,8},{11,10},{13,12},{15,14},{17,16},{19,... | collective-permute-start | bytes 11768 | tf_op jit(solution)/shard_map/ppermute | solution.py:27
  87.0 2.8 %while.14 = (s32[]{:T(128)}, f32[96,256]{1,0:T(8,128)S(1)}, s32[]{:T(128)}, f32[4,96,256]{2,1,0:T(8,128)}, s32[]{:T(128)}, /*index=5*/s32[]{:T(128)}) while((s32[]{:T(128)}, f32[96,256]{1,0:T(8,128)S(1)}, s32[]{:T(128)}, f32[4,96,256]{2,1,0:T(8,128)}, s32[]{:T(128)}, /*index=5*/s32[]{:T(128)}) %tuple.53), condition=%wide.region_2.3_spmd.clone, body=%wide.region_1.2_spmd.clone.sunk | while | flops 73732 | bytes 295013 | solution.py:41
  89.9 1.7 %collective-permute-done.16 = f32[10,98,1]{1,0,2:T(8,128)} collective-permute-done((f32[10,98,1]{1,0,2:T(8,128)}, f32[10,98,1]{1,0,2:T(8,128)}, u32[]{:S(2)}, u32[]{:S(2)}) %collective-permute-start.16) | collective-permute-done | bytes 3952 | tf_op jit(solution)/shard_map/ppermute | solution.py:27
  91.6 1.8 %copy.61 = f32[10,98,1]{2,1,0:T(8,128)} copy(f32[10,98,1]{1,0,2:T(8,128)} %collective-permute-done.16) | data formatting | bytes 7840 | tf_op jit(solution)/shard_map/ppermute | solution.py:27
  93.4 1.8 %copy.63 = f32[10,98,1]{2,1,0:T(8,128)} copy(f32[10,98,1]{1,0,2:T(8,128)} %collective-permute-done.17) | data formatting | bytes 7840 | tf_op jit(solution)/shard_map/ppermute | solution.py:26
  95.1 8.4 %subtract_divide_fusion = (f32[8,96,256]{2,1,0:T(8,128)}, f32[8,96,256]{2,1,0:T(8,128)}, f32[8,96,256]{2,1,0:T(8,128)}) fusion(f32[8]{0:T(128)S(1)} %copy-done.17, f32[8,96,256]{2,1,0:T(8,128)S(1)} %copy-done.1, pred[8,96,256]{2,1,0:T(8,128)(4,1)} %get-tuple-element.118, pred[8,96,256]{2,1,0:T(8,128)(4,1)} %get-tuple-element.117, ...), kind=kLoop, calls=%fused_computation.109 | loop fusion | flops 26148864 | bytes 8412512 | tf_op jit(solution)/shard_map/div | solution.py:110
  (90 shorter events, 13.7 us)
Async XLA Ops:
  1.6 13.3 %collective-permute-start.1 = (f32[1,96,256]{2,1,0:T(8,128)S(1)}, f32[1,96,256]{2,1,0:T(8,128)S(1)}, u32[]{:S(2)}, u32[]{:S(2)}) collective-permute-start(f32[1,96,256]{2,1,0:T(8,128)S(1)} %get-tuple-element.135), channel_id=1, source_target_pairs={{8,0},{16,8},{24,16},{9,1},{17,9},{25,17},{10,2},{18,10},{26,18},{... | collective-permute-start | bytes 294920 | tf_op jit(solution)/shard_map/ppermute | solution.py:27
  2.9 11.9 %collective-permute-start.3 = (f32[1,96,256]{2,1,0:T(8,128)S(1)}, f32[1,96,256]{2,1,0:T(8,128)S(1)}, u32[]{:S(2)}, u32[]{:S(2)}) collective-permute-start(f32[1,96,256]{2,1,0:T(8,128)S(1)} %get-tuple-element.136), channel_id=1, source_target_pairs={{0,8},{8,16},{16,24},{1,9},{9,17},{17,25},{2,10},{10,18},{18,26},{... | collective-permute-start | bytes 294920 | tf_op jit(solution)/shard_map/ppermute | solution.py:26
  5.9 8.9 %copy-start = (f32[8,96,256]{2,1,0:T(8,128)S(1)}, f32[8,96,256]{2,1,0:T(8,128)}, u32[]{:S(2)}) copy-start(f32[8,96,256]{2,1,0:T(8,128)} %param.6) | copy-start | bytes 2359300
  9.0 11.8 %collective-permute-start.2 = (f32[1,96,256]{2,1,0:T(8,128)S(1)}, f32[1,96,256]{2,1,0:T(8,128)S(1)}, u32[]{:S(2)}, u32[]{:S(2)}) collective-permute-start(f32[1,96,256]{2,1,0:T(8,128)S(1)} %get-tuple-element.133), channel_id=1, source_target_pairs={{0,8},{8,16},{16,24},{1,9},{9,17},{17,25},{2,10},{10,18},{18,26},{... | collective-permute-start | bytes 294920 | tf_op jit(solution)/shard_map/ppermute | solution.py:26
  13.5 7.4 %collective-permute-start = (f32[1,96,256]{2,1,0:T(8,128)S(1)}, f32[1,96,256]{2,1,0:T(8,128)S(1)}, u32[]{:S(2)}, u32[]{:S(2)}) collective-permute-start(f32[1,96,256]{2,1,0:T(8,128)S(1)} %get-tuple-element.134), channel_id=1, source_target_pairs={{8,0},{16,8},{24,16},{9,1},{17,9},{25,17},{10,2},{18,10},{26,18},{... | collective-permute-start | bytes 294920 | tf_op jit(solution)/shard_map/ppermute | solution.py:27
  14.8 6.1 %copy-start.11 = (f32[1,96,256]{2,1,0:T(8,128)}, f32[1,96,256]{2,1,0:T(8,128)S(1)}, u32[]{:S(2)}) copy-start(f32[1,96,256]{2,1,0:T(8,128)S(1)} %collective-permute-done.3) | copy-start | bytes 294916
  14.9 11.9 %copy-start.10 = (f32[1,96,256]{2,1,0:T(8,128)}, f32[1,96,256]{2,1,0:T(8,128)S(1)}, u32[]{:S(2)}) copy-start(f32[1,96,256]{2,1,0:T(8,128)S(1)} %collective-permute-done.1) | copy-start | bytes 294916
  14.9 12.1 %copy-start.2 = (f32[10,96,256]{2,1,0:T(8,128)}, f32[10,96,256]{2,1,0:T(8,128)S(1)}, u32[]{:S(2)}) copy-start(f32[10,96,256]{2,1,0:T(8,128)S(1)} %constant_dynamic-update-slice_fusion) | copy-start | bytes 2949124
  15.0 11.8 %collective-permute-start.5 = (f32[10,1,256]{2,0,1:T(8,128)S(1)}, f32[10,1,256]{2,0,1:T(8,128)S(1)}, u32[]{:S(2)}, u32[]{:S(2)}) collective-permute-start(f32[10,1,256]{2,0,1:T(8,128)S(1)} %copy.65), channel_id=1, source_target_pairs={{2,0},{4,2},{6,4},{3,1},{5,3},{7,5},{10,8},{12,10},{14,12},{11,9},... | collective-permute-start | bytes 30728 | tf_op jit(solution)/shard_map/ppermute | solution.py:27
  16.3 10.5 %collective-permute-start.7 = (f32[10,1,256]{2,0,1:T(8,128)S(1)}, f32[10,1,256]{2,0,1:T(8,128)S(1)}, u32[]{:S(2)}, u32[]{:S(2)}) collective-permute-start(f32[10,1,256]{2,0,1:T(8,128)S(1)} %copy.67), channel_id=1, source_target_pairs={{0,2},{2,4},{4,6},{1,3},{3,5},{5,7},{8,10},{10,12},{12,14},{9,11},... | collective-permute-start | bytes 30728 | tf_op jit(solution)/shard_map/ppermute | solution.py:26
  20.9 23.3 %copy-start.7 = (f32[1,96,256]{2,1,0:T(8,128)}, f32[1,96,256]{2,1,0:T(8,128)S(1)}, u32[]{:S(2)}) copy-start(f32[1,96,256]{2,1,0:T(8,128)S(1)} %collective-permute-done) | copy-start | bytes 294916
  20.9 11.9 %collective-permute-start.4 = (f32[10,1,256]{2,0,1:T(8,128)S(1)}, f32[10,1,256]{2,0,1:T(8,128)S(1)}, u32[]{:S(2)}, u32[]{:S(2)}) collective-permute-start(f32[10,1,256]{2,0,1:T(8,128)S(1)} %copy.64), channel_id=1, source_target_pairs={{2,0},{4,2},{6,4},{3,1},{5,3},{7,5},{10,8},{12,10},{14,12},{11,9},... | collective-permute-start | bytes 30728 | tf_op jit(solution)/shard_map/ppermute | solution.py:27
  22.2 10.6 %collective-permute-start.6 = (f32[10,1,256]{2,0,1:T(8,128)S(1)}, f32[10,1,256]{2,0,1:T(8,128)S(1)}, u32[]{:S(2)}, u32[]{:S(2)}) collective-permute-start(f32[10,1,256]{2,0,1:T(8,128)S(1)} %copy.66), channel_id=1, source_target_pairs={{0,2},{2,4},{4,6},{1,3},{3,5},{5,7},{8,10},{10,12},{12,14},{9,11},... | collective-permute-start | bytes 30728 | tf_op jit(solution)/shard_map/ppermute | solution.py:26
  28.1 12.9 %collective-permute-start.11 = (f32[10,98,1]{1,0,2:T(8,128)S(1)}, f32[10,98,1]{1,0,2:T(8,128)S(1)}, u32[]{:S(2)}, u32[]{:S(2)}) collective-permute-start(f32[10,98,1]{1,0,2:T(8,128)S(1)} %copy.52), channel_id=1, source_target_pairs={{0,1},{2,3},{4,5},{6,7},{8,9},{10,11},{12,13},{14,15},{16,17},{18,... | collective-permute-start | bytes 11768 | tf_op jit(solution)/shard_map/ppermute | solution.py:26
  31.5 8.4 %collective-permute-start.9 = (f32[10,98,1]{1,0,2:T(8,128)S(1)}, f32[10,98,1]{1,0,2:T(8,128)S(1)}, u32[]{:S(2)}, u32[]{:S(2)}) collective-permute-start(f32[10,98,1]{1,0,2:T(8,128)S(1)} %copy.48), channel_id=1, source_target_pairs={{1,0},{3,2},{5,4},{7,6},{9,8},{11,10},{13,12},{15,14},{17,16},{19,... | collective-permute-start | bytes 11768 | tf_op jit(solution)/shard_map/ppermute | solution.py:27
  33.8 8.3 %collective-permute-start.8 = (f32[10,98,1]{1,0,2:T(8,128)S(1)}, f32[10,98,1]{1,0,2:T(8,128)S(1)}, u32[]{:S(2)}, u32[]{:S(2)}) collective-permute-start(f32[10,98,1]{1,0,2:T(8,128)S(1)} %copy.44), channel_id=1, source_target_pairs={{1,0},{3,2},{5,4},{7,6},{9,8},{11,10},{13,12},{15,14},{17,16},{19,... | collective-permute-start | bytes 11768 | tf_op jit(solution)/shard_map/ppermute | solution.py:27
  35.4 7.7 %collective-permute-start.10 = (f32[10,98,1]{1,0,2:T(8,128)S(1)}, f32[10,98,1]{1,0,2:T(8,128)S(1)}, u32[]{:S(2)}, u32[]{:S(2)}) collective-permute-start(f32[10,98,1]{1,0,2:T(8,128)S(1)} %copy.50), channel_id=1, source_target_pairs={{0,1},{2,3},{4,5},{6,7},{8,9},{10,11},{12,13},{14,15},{16,17},{18,... | collective-permute-start | bytes 11768 | tf_op jit(solution)/shard_map/ppermute | solution.py:26
  44.2 10.2 %copy-start.1 = (f32[8,96,256]{2,1,0:T(8,128)S(1)}, f32[8,96,256]{2,1,0:T(8,128)}, u32[]{:S(2)}) copy-start(f32[8,96,256]{2,1,0:T(8,128)} %param.7) | copy-start | bytes 2359300
  44.2 10.2 %copy-start.4 = (pred[8,96,256]{2,1,0:T(8,128)(4,1)S(1)}, pred[8,96,256]{2,1,0:T(8,128)(4,1)}, u32[]{:S(2)}) copy-start(pred[8,96,256]{2,1,0:T(8,128)(4,1)} %get-tuple-element.116) | copy-start | bytes 589828
  44.2 10.2 %copy-start.5 = (pred[8,96,256]{2,1,0:T(8,128)(4,1)S(1)}, pred[8,96,256]{2,1,0:T(8,128)(4,1)}, u32[]{:S(2)}) copy-start(pred[8,96,256]{2,1,0:T(8,128)(4,1)} %get-tuple-element.117) | copy-start | bytes 589828
  44.2 10.2 %copy-start.6 = (pred[8,96,256]{2,1,0:T(8,128)(4,1)S(1)}, pred[8,96,256]{2,1,0:T(8,128)(4,1)}, u32[]{:S(2)}) copy-start(pred[8,96,256]{2,1,0:T(8,128)(4,1)} %get-tuple-element.118) | copy-start | bytes 589828
  44.2 10.2 %copy-start.17 = (f32[8]{0:T(128)S(1)}, f32[8]{0:T(128)}, u32[]{:S(2)}) copy-start(f32[8]{0:T(128)} %param.9) | copy-start | bytes 100
  51.7 4.1 %collective-permute-start.13 = (f32[1,96,256]{2,1,0:T(8,128)S(1)}, f32[1,96,256]{2,1,0:T(8,128)S(1)}, u32[]{:S(2)}, u32[]{:S(2)}) collective-permute-start(f32[1,96,256]{2,1,0:T(8,128)S(1)} %get-tuple-element.131), channel_id=1, source_target_pairs={{0,8},{8,16},{16,24},{1,9},{9,17},{17,25},{2,10},{10,18},{18,26},{... | collective-permute-start | bytes 294920 | tf_op jit(solution)/shard_map/ppermute | solution.py:26
  53.0 6.2 %collective-permute-start.12 = (f32[1,96,256]{2,1,0:T(8,128)S(1)}, f32[1,96,256]{2,1,0:T(8,128)S(1)}, u32[]{:S(2)}, u32[]{:S(2)}) collective-permute-start(f32[1,96,256]{2,1,0:T(8,128)S(1)} %get-tuple-element.132), channel_id=1, source_target_pairs={{8,0},{16,8},{24,16},{9,1},{17,9},{25,17},{10,2},{18,10},{26,18},{... | collective-permute-start | bytes 294920 | tf_op jit(solution)/shard_map/ppermute | solution.py:27
  55.9 19.4 %copy-start.8 = (f32[1,96,256]{2,1,0:T(8,128)}, f32[1,96,256]{2,1,0:T(8,128)S(1)}, u32[]{:S(2)}) copy-start(f32[1,96,256]{2,1,0:T(8,128)S(1)} %collective-permute-done.13) | copy-start | bytes 294916
  59.2 16.0 %copy-start.9 = (f32[1,96,256]{2,1,0:T(8,128)}, f32[1,96,256]{2,1,0:T(8,128)S(1)}, u32[]{:S(2)}) copy-start(f32[1,96,256]{2,1,0:T(8,128)S(1)} %collective-permute-done.12) | copy-start | bytes 294916
  60.5 14.8 %collective-permute-start.14 = (f32[10,1,256]{2,0,1:T(8,128)}, f32[10,1,256]{2,0,1:T(8,128)}, u32[]{:S(2)}, u32[]{:S(2)}) collective-permute-start(f32[10,1,256]{2,0,1:T(8,128)} %copy.68), channel_id=1, source_target_pairs={{2,0},{4,2},{6,4},{3,1},{5,3},{7,5},{10,8},{12,10},{14,12},{11,9},... | collective-permute-start | bytes 30728 | tf_op jit(solution)/shard_map/ppermute | solution.py:27
  61.8 14.2 %collective-permute-start.15 = (f32[10,1,256]{2,0,1:T(8,128)}, f32[10,1,256]{2,0,1:T(8,128)}, u32[]{:S(2)}, u32[]{:S(2)}) collective-permute-start(f32[10,1,256]{2,0,1:T(8,128)} %copy.69), channel_id=1, source_target_pairs={{0,2},{2,4},{4,6},{1,3},{3,5},{5,7},{8,10},{10,12},{12,14},{9,11},... | collective-permute-start | bytes 30728 | tf_op jit(solution)/shard_map/ppermute | solution.py:26
  76.0 3.0 %copy-start.15 = (f32[10,1,256]{2,1,0:T(1,128)}, f32[10,1,256]{2,1,0:T(1,128)S(1)}, u32[]{:S(2)}) copy-start(f32[10,1,256]{2,1,0:T(1,128)S(1)} %copy.55) | copy-start | bytes 30724
  76.7 2.2 %copy-start.16 = (f32[10,1,256]{2,1,0:T(1,128)}, f32[10,1,256]{2,1,0:T(1,128)S(1)}, u32[]{:S(2)}) copy-start(f32[10,1,256]{2,1,0:T(1,128)S(1)} %copy.57) | copy-start | bytes 30724
  82.8 10.5 %collective-permute-start.17 = (f32[10,98,1]{1,0,2:T(8,128)}, f32[10,98,1]{1,0,2:T(8,128)}, u32[]{:S(2)}, u32[]{:S(2)}) collective-permute-start(f32[10,98,1]{1,0,2:T(8,128)} %copy.62), channel_id=1, source_target_pairs={{0,1},{2,3},{4,5},{6,7},{8,9},{10,11},{12,13},{14,15},{16,17},{18,... | collective-permute-start | bytes 11768 | tf_op jit(solution)/shard_map/ppermute | solution.py:26
  85.7 5.8 %collective-permute-start.16 = (f32[10,98,1]{1,0,2:T(8,128)}, f32[10,98,1]{1,0,2:T(8,128)}, u32[]{:S(2)}, u32[]{:S(2)}) collective-permute-start(f32[10,98,1]{1,0,2:T(8,128)} %copy.60), channel_id=1, source_target_pairs={{1,0},{3,2},{5,4},{7,6},{9,8},{11,10},{13,12},{15,14},{17,16},{19,... | collective-permute-start | bytes 11768 | tf_op jit(solution)/shard_map/ppermute | solution.py:27
  (4 other events, 2.7 us)
where the time goes:
time: 105 us; the launch traced here: 103 us
  starting transfers between devices  45.6 us (43%)
  other arithmetic  23.6 us (22%)
  local copies, waits for them, and re-layouts  19.6 us (19%)
  blocking collectives  8.31 us (8%)
  waiting for transfers between devices  5.09 us (5%)
  between operations  1.22 us (1%)
    ppermute x9, starting transfers between devices, padded_2(): before = lax.ppermute(last, axis, up)  33.9 us
    ppermute x9, starting transfers between devices, padded_2(): after = lax.ppermute(leading, axis, down)  11.6 us
    div x1, other arithmetic, body(): thickness_new = solid / (1.0 - porosity_new)  8.37 us
    all_gather x1, blocking collectives, carried_in(): pieces = lax.all_gather(value, axis)  8.31 us
    add x1, other arithmetic, body(): middle = pressure + first_step  7.51 us
    ppermute x9, waiting for transfers between devices, padded_2(): after = lax.ppermute(leading, axis, down)  5.07 us
    slice x7, local copies, waits for them, and re-layouts, padded_2(): leading = lax.slice_in_dim(array, 0, width, axis=dim)  5.02 us
    ppermute x6, local copies, waits for them, and re-layouts, padded_2(): before = lax.ppermute(last, axis, up)  4.63 us
  transfers between devices with their start and end apart: 18, of which 2 were waited for; matrix products, arithmetic and copies ran while one was open for 14% of the time, Pallas kernels for 0%

commit v1 on v0

v1 whole, which is shorter than its diff:
```python
import functools
import math

import jax
import jax.numpy as jnp
from jax import lax
from jax.experimental import pallas as pl
from jax.experimental.pallas import tpu as pltpu
from jax.sharding import PartitionSpec as P

PHI_SURFACE = (0.45, 0.55, 0.65, 0.4)
ATHY_RATE = (0.25, 0.45, 0.8, 0.35)
MOB_BASE = (1.0, 0.0, -1.5, -0.5)
MOB_SLOPE = (6.0, 5.0, 8.0, 4.0)
GRAIN_DENSITY = (2.65, 2.68, 2.72, 2.71)
WATER_DENSITY = 1.03
SPECTRUM_MID = 1.0
SPECTRUM_HALF = 0.95
SIGMA_RATIO = SPECTRUM_MID / SPECTRUM_HALF
RHO_FIRST = 1.0 / SIGMA_RATIO
RHO_SECOND = 1.0 / (2.0 * SIGMA_RATIO - RHO_FIRST)
STEP_KEEP = RHO_SECOND * RHO_FIRST
STEP_RES = 2.0 * RHO_SECOND / SPECTRUM_HALF

HALF_BASE = tuple(-(b - 0.35 * s) - math.log(2.0) for b, s in zip(MOB_BASE, MOB_SLOPE))
HALF_SLOPE = tuple(-s for s in MOB_SLOPE)
GRAIN_LESS = tuple(g - WATER_DENSITY for g in GRAIN_DENSITY)
ATHY_NEG = tuple(-a for a in ATHY_RATE)
OUTSIDE = 2.0e38

MESH = pl.DeviceIdType.MESH
PAD = 8
ROWS = 16
Z_P, Z_H, X_1, Y_1, Z_Q, X_Q, Y_Q, CHAIN = 0, 2, 4, 6, 8, 10, 12, 14
MESSAGES = 15


def rec(x):
    r = pl.reciprocal(x, approx=True)
    return r * (2.0 - x * r)


def classes(lith):
    return lith >= 2, (lith & 1) == 1


def pick(cls, table):
    high, odd = cls
    a, b, c, d = (jnp.float32(t) for t in table)
    return jnp.where(high, jnp.where(odd, d, c), jnp.where(odd, b, a))


def kernel(sizes, p_hbm, por_hbm, lit_hbm, solid, pn_out, phi_out, thick_out,
           pv, hv, qv, tz, tx, tym, typ, rd, ob, por, lit, col, col_send, above,
           xs, xr, ys, yr, xqs, xqr, yqs, yqr, load_sem, send_sem, recv_sem):
    nz, nx, ny = por.shape
    axes = ("slab", "mapx", "mapy")
    me = {a: lax.axis_index(a) for a in axes}
    has_lo = {a: me[a] > 0 for a in axes}
    has_hi = {a: me[a] < sizes[a] - 1 for a in axes}
    peers = sum(jnp.where(f, 1, 0) for flags in (has_lo, has_hi) for f in flags.values())
    inner = pl.ds(PAD, nx)

    loads = [
        pltpu.make_async_copy(por_hbm, por, load_sem.at[0]),
        pltpu.make_async_copy(lit_hbm, lit, load_sem.at[1]),
        pltpu.make_async_copy(p_hbm, pv.at[pl.ds(1, nz), inner, :], load_sem.at[2]),
    ]
    for c in loads:
        c.start()

    barrier = pltpu.get_barrier_semaphore()
    for a in axes:
        @pl.when(has_lo[a])
        def _():
            pl.semaphore_signal(barrier, inc=1, device_id={a: me[a] - 1}, device_id_type=MESH)

        @pl.when(has_hi[a])
        def _():
            pl.semaphore_signal(barrier, inc=1, device_id={a: me[a] + 1}, device_id_type=MESH)

    def message(k, axis, up, src, dst):
        target = me[axis] + 1 if up else me[axis] - 1
        return pltpu.make_async_remote_copy(
            src_ref=src, dst_ref=dst, send_sem=send_sem.at[k], recv_sem=recv_sem.at[k],
            device_id={axis: target}, device_id_type=MESH)

    def pair(k, axis, src_up, dst_up, src_down, dst_down):
        return [(k, axis, True, src_up, dst_up), (k + 1, axis, False, src_down, dst_down)]

    z_lo, z_hi = 0, nz + 1
    groups = {
        Z_P: pair(Z_P, "slab", p_hbm.at[nz - 1], pv.at[z_lo, inner, :],
                  p_hbm.at[0], pv.at[z_hi, inner, :]),
        Z_H: pair(Z_H, "slab", hv.at[nz, inner, :], hv.at[z_lo, inner, :],
                  hv.at[1, inner, :], hv.at[z_hi, inner, :]),
        X_1: pair(X_1, "mapx", xs.at[0], xr.at[0], xs.at[1], xr.at[1]),
        Y_1: pair(Y_1, "mapy", ys.at[0], yr.at[0], ys.at[1], yr.at[1]),
        Z_Q: pair(Z_Q, "slab", qv.at[nz, inner, :], qv.at[z_lo, inner, :],
                  qv.at[1, inner, :], qv.at[z_hi, inner, :]),
        X_Q: pair(X_Q, "mapx", xqs.at[0], xqr.at[0], xqs.at[1], xqr.at[1]),
        Y_Q: pair(Y_Q, "mapy", yqs.at[0], yqr.at[0], yqs.at[1], yqr.at[1]),
    }

    def start(group):
        for k, axis, up, src, dst in groups[group]:
            @pl.when(has_hi[axis] if up else has_lo[axis])
            def _():
                message(k, axis, up, src, dst).start()

    def arrived(group):
        for k, axis, up, src, dst in groups[group]:
            @pl.when(has_lo[axis] if up else has_hi[axis])
            def _():
                message(k, axis, up, src, dst).wait_recv()

    def sent(group):
        for k, axis, up, src, dst in groups[group]:
            @pl.when(has_hi[axis] if up else has_lo[axis])
            def _():
                message(k, axis, up, src, dst).wait_send()

    lane_y = lax.broadcasted_iota(jnp.int32, (nx, 128), 1)

    for axis, flags in (("lo", has_lo), ("hi", has_hi)):
        side = 0 if axis == "lo" else 1
        layer = z_lo if side == 0 else z_hi

        @pl.when(jnp.logical_not(flags["slab"]))
        def _():
            pv[layer, inner, :] = jnp.zeros((nx, ny), jnp.float32)
            qv[layer, inner, :] = jnp.zeros((nx, ny), jnp.float32)
            hv[layer, inner, :] = jnp.full((nx, ny), OUTSIDE, jnp.float32)
            if side == 0:
                above[...] = jnp.zeros((nx, ny), jnp.float32)

        @pl.when(jnp.logical_not(flags["mapx"]))
        def _():
            xr[side, pl.ds(0, nz), :] = jnp.zeros((nz, ny), jnp.float32)
            xr[side, pl.ds(nz, nz), :] = jnp.full((nz, ny), OUTSIDE, jnp.float32)
            xqr[side] = jnp.zeros((nz, ny), jnp.float32)

        @pl.when(jnp.logical_not(flags["mapy"]))
        def _():
            yr[side] = jnp.where(lane_y < nz, jnp.float32(0.0), jnp.float32(OUTSIDE))
            yqr[side] = jnp.zeros((nx, 128), jnp.float32)

    pl.semaphore_wait(barrier, peers)

    start(Z_P)
    loads[0].wait()
    loads[1].wait()

    def half_inverse(z):
        for r in range(0, nx, 32):
            rows = pl.ds(r, 32)
            cls = classes(lit[z, rows, :])
            hv[z + 1, pl.ds(PAD + r, 32), :] = jnp.exp(
                pick(cls, HALF_BASE) + pick(cls, HALF_SLOPE) * por[z, rows, :])

    half_inverse(0)
    half_inverse(nz - 1)
    start(Z_H)
    lax.fori_loop(1, nz - 1, lambda z, c: (half_inverse(z), c)[1], 0)
    loads[2].wait()

    def face_x(src, dst, offset):
        for side, row in ((0, PAD + nx - 1), (1, PAD)):
            for z in range(nz):
                dst[side, pl.ds(offset + z, 1), :] = src[z + 1, pl.ds(row, 1), :]

    def face_y(srcs, dst):
        for side in range(2):
            for r in range(0, nx, 32):
                acc = jnp.zeros((32, 128), jnp.float32)
                lane = lane_y[:32]
                for i, src in enumerate(srcs):
                    for z in range(nz):
                        k = i * nz + z
                        if side == 0:
                            col_ = src[z + 1, pl.ds(PAD + r, 32), pl.ds(ny - 128, 128)]
                            moved = pltpu.roll(col_, k + 1, 1)
                        else:
                            col_ = src[z + 1, pl.ds(PAD + r, 32), pl.ds(0, 128)]
                            moved = pltpu.roll(col_, k, 1) if k else col_
                        acc = jnp.where(lane == k, moved, acc)
                dst[side, pl.ds(r, 32), :] = acc

    face_x(pv, xs, 0)
    face_x(hv, xs, nz)
    start(X_1)
    face_y((pv, hv), ys)
    start(Y_1)

    for r in range(0, nx, 32):
        rows = pl.ds(r, 32)

        def add_layer(z, total):
            cls = classes(lit[z, rows, :])
            load = (pick(cls, GRAIN_LESS) + WATER_DENSITY * rec(1.0 - por[z, rows, :])) * solid[z]
            ob[z, rows, :] = total + 0.5 * load
            return total + load

        col[rows, :] = lax.fori_loop(0, nz, add_layer, jnp.zeros((32, ny), jnp.float32))

    def chain(src):
        return message(CHAIN, "slab", True, src, above)

    @pl.when(me["slab"] == 0)
    def _():
        col_send[...] = col[...]
        chain(col_send).start()

    def forward():
        chain(col_send).wait_recv()
        col_send[...] = col[...] + above[...]
        chain(col_send).start()

    @pl.when(me["slab"] == 1)
    def _():
        forward()

    def spread_x(src, offset, dst):
        for side, row in ((0, PAD - 1), (1, PAD + nx)):
            for z in range(nz):
                dst[z + 1, pl.ds(row, 1), :] = src[side, pl.ds(offset + z, 1), :]

    arrived(X_1)
    spread_x(xr, 0, pv)
    spread_x(xr, nz, hv)
    arrived(Y_1)
    arrived(Z_P)
    arrived(Z_H)

    lane = lax.broadcasted_iota(jnp.int32, (ROWS, ny), 1)

    def beside_y(value, halo, index, r):
        lo = pltpu.roll(halo[0, pl.ds(r, ROWS), :], lax.rem(128 - index, 128), 1)
        hi = pltpu.roll(halo[1, pl.ds(r, ROWS), :], 127 - index, 1)
        wide = lambda v: jnp.concatenate([v] * (ny // 128), axis=1)
        before = jnp.where(lane == 0, wide(lo), pltpu.roll(value, 1, 1))
        after = jnp.where(lane == ny - 1, wide(hi), pltpu.roll(value, ny - 1, 1))
        return before, after

    def first(z):
        for r in range(0, nx, ROWS):
            at = lambda ref, dz, dx: ref[z + 1 + dz, pl.ds(PAD + r + dx, ROWS), :]
            rows = pl.ds(r, ROWS)
            h, p = at(hv, 0, 0), at(pv, 0, 0)
            h_before, h_after = beside_y(h, yr, nz + z, r)
            p_before, p_after = beside_y(p, yr, z, r)
            t_zm, t_zp = rec(h + at(hv, -1, 0)), rec(h + at(hv, 1, 0))
            t_xm, t_xp = rec(h + at(hv, 0, -1)), rec(h + at(hv, 0, 1))
            t_ym, t_yp = rec(h + h_before), rec(h + h_after)
            diag = 1.0 + ((t_zm + t_zp) + (t_xm + t_xp) + (t_ym + t_yp))
            inv = rec(diag)
            total = (p + (t_zm * at(pv, -1, 0) + t_zp * at(pv, 1, 0))
                     + (t_xm * at(pv, 0, -1) + t_xp * at(pv, 0, 1))
                     + (t_ym * p_before + t_yp * p_after))
            tz[z, rows, :] = t_zm
            tz[z + 1, rows, :] = t_zp
            tx[z, rows, :] = t_xm
            if r + ROWS == nx:
                tx[z, pl.ds(nx, 1), :] = t_xp[ROWS - 1:, :]
            tym[z, rows, :] = t_ym
            typ[z, rows, :] = t_yp
            rd[z, rows, :] = inv
            qv[z + 1, pl.ds(PAD + r, ROWS), :] = total * inv

    first(0)
    first(nz - 1)
    start(Z_Q)
    lax.fori_loop(1, nz - 1, lambda z, c: (first(z), c)[1], 0)
    face_x(qv, xqs, 0)
    start(X_Q)
    face_y((qv,), yqs)
    start(Y_Q)

    @pl.when(me["slab"] == 2)
    def _():
        forward()

    @pl.when(me["slab"] == 3)
    def _():
        chain(col_send).wait_recv()

    arrived(X_Q)
    spread_x(xqr, 0, qv)
    arrived(Y_Q)
    arrived(Z_Q)

    def second(z, carry):
        for r in range(0, nx, ROWS):
            at = lambda ref, dz, dx: ref[z + 1 + dz, pl.ds(PAD + r + dx, ROWS), :]
            rows = pl.ds(r, ROWS)
            p, q = at(pv, 0, 0), at(qv, 0, 0)
            q_before, q_after = beside_y(q, yqr, z, r)
            total = (p + (tz[z, rows, :] * at(qv, -1, 0) + tz[z + 1, rows, :] * at(qv, 1, 0))
                     + (tx[z, rows, :] * at(qv, 0, -1) + tx[z, pl.ds(r + 1, ROWS), :] * at(qv, 0, 1))
                     + (tym[z, rows, :] * q_before + typ[z, rows, :] * q_after))
            pn = q + STEP_KEEP * (q - p) + STEP_RES * (total * rd[z, rows, :] - q)
            stress = jnp.maximum(above[rows, :] + ob[z, rows, :] - pn, 0.0)
            cls = classes(lit[z, rows, :])
            phi = pick(cls, PHI_SURFACE) * jnp.exp(pick(cls, ATHY_NEG) * stress)
            pn_out[z, rows, :] = pn
            phi_out[z, rows, :] = phi
            thick_out[z, rows, :] = solid[z] * rec(1.0 - phi)
        return carry

    lax.fori_loop(0, nz, second, 0)

    for group in groups:
        sent(group)

    @pl.when(has_hi["slab"])
    def _():
        chain(col_send).wait_send()


def body(sizes, pressure, porosity, lithology, layer_solid):
    nz, nx, ny = pressure.shape
    f32 = jnp.float32
    block = pltpu.VMEM((nz, nx, ny), f32)
    padded = pltpu.VMEM((nz + 2, nx + 2 * PAD, ny), f32)
    plane = pltpu.VMEM((nx, ny), f32)
    out = jax.ShapeDtypeStruct((nz, nx, ny), f32)
    vmem = pl.BlockSpec(memory_space=pltpu.VMEM)
    return pl.pallas_call(
        functools.partial(kernel, sizes),
        out_shape=(out, out, out),
        in_specs=[pl.BlockSpec(memory_space=pl.ANY)] * 3 + [pl.BlockSpec(memory_space=pltpu.SMEM)],
        out_specs=(vmem, vmem, vmem),
        scratch_shapes=[
            padded, padded, padded,
            pltpu.VMEM((nz + 1, nx, ny), f32), pltpu.VMEM((nz, nx + PAD, ny), f32),
            block, block, block, block, block, pltpu.VMEM((nz, nx, ny), jnp.int32),
            plane, plane, plane,
            pltpu.VMEM((2, 2 * nz, ny), f32), pltpu.VMEM((2, 2 * nz, ny), f32),
            pltpu.VMEM((2, nx, 128), f32), pltpu.VMEM((2, nx, 128), f32),
            pltpu.VMEM((2, nz, ny), f32), pltpu.VMEM((2, nz, ny), f32),
            pltpu.VMEM((2, nx, 128), f32), pltpu.VMEM((2, nx, 128), f32),
            pltpu.SemaphoreType.DMA((3,)),
            pltpu.SemaphoreType.DMA((MESSAGES,)),
            pltpu.SemaphoreType.DMA((MESSAGES,)),
        ],
        compiler_params=pltpu.CompilerParams(
            collective_id=0, has_side_effects=True, vmem_limit_bytes=32 * 2**20),
        name="basin",
    )(pressure, porosity, lithology, layer_solid)


def solution(mesh):
    sizes = dict(mesh.shape)
    spec = P("slab", "mapx", "mapy")
    return jax.shard_map(
        functools.partial(body, sizes), mesh=mesh,
        in_specs=(spec, spec, spec, P("slab")), out_specs=(spec, spec, spec), check_vma=False)
```

time: 105 us -> 23.1 us (0.22); the launches traced: 103 us -> 22.9 us
  starting transfers between devices: 45.6 us -> 0 us
  other arithmetic: 23.6 us -> 0 us
  Pallas kernels: 0 us -> 15.6 us
  local copies, waits for them, and re-layouts: 19.6 us -> 6.69 us
  blocking collectives: 8.31 us -> 0 us
  waiting for transfers between devices: 5.09 us -> 0 us
    ppermute x18 -> x0, starting transfers between devices: 45.6 us -> none  [the longest x9 33.9 us: padded_2(): before = lax.ppermute(last, axis, up)]
    pallas_call x0 -> x1, Pallas kernels: none -> 15.6 us  [body(): pl.pallas_call(functools.partial(kernel, sizes), out_shape=(out, out, out...]
    ppermute x12 -> x0, local copies, waits for them, and re-layouts: 9.25 us -> none  [the longest x6 4.63 us: padded_2(): before = lax.ppermute(last, axis, up)]
    div x1 -> x0, other arithmetic: 8.37 us -> none  [body(): thickness_new = solid / (1.0 - porosity_new)]
    all_gather x1 -> x0, blocking collectives: 8.31 us -> none  [carried_in(): pieces = lax.all_gather(value, axis)]
    slice x14 -> x0, local copies, waits for them, and re-layouts: 7.63 us -> none  [the longest x7 5.02 us: padded_2(): leading = lax.slice_in_dim(array, 0, width, axis=dim)]
    add x1 -> x0, other arithmetic: 7.51 us -> none  [body(): middle = pressure + first_step]
    ppermute x18 -> x0, waiting for transfers between devices: 5.09 us -> none  [the longest x9 5.07 us: padded_2(): after = lax.ppermute(leading, axis, down)]
  transfers between devices with their start and end apart: 18 -> 0, of which waited for: 2 -> 0; matrix products, arithmetic and copies ran while one was open for 14% -> 0% of each run, Pallas kernels for 0% -> 0%
where the time goes in v1:
time: 23.1 us; the launch traced here: 22.9 us
  Pallas kernels  15.6 us (68%)
  local copies, waits for them, and re-layouts  6.69 us (29%)
  between operations  0.65 us (3%)
    pallas_call x1, Pallas kernels, body(): pl.pallas_call(functools.partial(kernel, sizes), out_shape=(out, out, out...  15.6 us
    unnamed x11, local copies, waits for them, and re-layouts  6.69 us

profile of v1, /device:TPU:0, one launch (start us, length us, event | category | flops | bytes accessed | tf_op | source)
XLA Modules:
  0.0 22.9 jit_solution(13898089928260951402)
XLA Ops:
  0.6 0.0 copy-start
  0.6 1.1 %copy-done = f32[8,96,256]{2,1,0:T(8,128)S(1)} copy-done((f32[8,96,256]{2,1,0:T(8,128)S(1)}, f32[8,96,256]{2,1,0:T(8,128)}, u32[]{:S(2)}) %copy-start) | copy-done | bytes 786456
  1.8 0.0 copy-start.1
  1.8 1.1 %copy-done.1 = f32[8,96,256]{2,1,0:T(8,128)S(1)} copy-done((f32[8,96,256]{2,1,0:T(8,128)S(1)}, f32[8,96,256]{2,1,0:T(8,128)}, u32[]{:S(2)}) %copy-start.1) | copy-done | bytes 786456
  2.9 0.0 copy-start.2
  2.9 1.1 %copy-done.2 = s32[8,96,256]{2,1,0:T(8,128)S(1)} copy-done((s32[8,96,256]{2,1,0:T(8,128)S(1)}, s32[8,96,256]{2,1,0:T(8,128)}, u32[]{:S(2)}) %copy-start.2) | copy-done | bytes 786456
  4.0 0.0 copy-start.3
  4.0 0.7 %copy-done.3 = f32[8]{0:T(128)S(1)} copy-done((f32[8]{0:T(128)S(1)}, f32[8]{0:T(128)}, u32[]{:S(2)}) %copy-start.3) | copy-done | bytes 56
  4.7 15.6 %basin.1 = (f32[8,96,256]{2,1,0:T(8,128)S(1)}, f32[8,96,256]{2,1,0:T(8,128)S(1)}, f32[8,96,256]{2,1,0:T(8,128)S(1)}) custom-call(f32[8,96,256]{2,1,0:T(8,128)S(1)} %copy-done, f32[8,96,256]{2,1,0:T(8,128)S(1)} %copy-done.1, s32[8,96,256]{2,1,0:T(8,128)S(1)} %copy-done.2, f32[8]{0:T(128)S(1)} %copy-done.3), custom_call_target="tpu_custom_call" | custom-call | tf_op jit(solution)/shard_map/basin/pallas_call | solution.py:328
  20.3 0.9 %copy.10 = f32[8,96,256]{2,1,0:T(8,128)} copy(f32[8,96,256]{2,1,0:T(8,128)S(1)} %get-tuple-element.6) | data formatting | bytes 1572864
  21.1 0.9 %copy.11 = f32[8,96,256]{2,1,0:T(8,128)} copy(f32[8,96,256]{2,1,0:T(8,128)S(1)} %get-tuple-element.7) | data formatting | bytes 1572864
  22.0 0.9 %copy.12 = f32[8,96,256]{2,1,0:T(8,128)} copy(f32[8,96,256]{2,1,0:T(8,128)S(1)} %get-tuple-element.8) | data formatting | bytes 1572864
Async XLA Ops:
  0.6 1.1 %copy-start = (f32[8,96,256]{2,1,0:T(8,128)S(1)}, f32[8,96,256]{2,1,0:T(8,128)}, u32[]{:S(2)}) copy-start(f32[8,96,256]{2,1,0:T(8,128)} %p_hbm.1) | copy-start | bytes 2359300
  1.8 1.1 %copy-start.1 = (f32[8,96,256]{2,1,0:T(8,128)S(1)}, f32[8,96,256]{2,1,0:T(8,128)}, u32[]{:S(2)}) copy-start(f32[8,96,256]{2,1,0:T(8,128)} %por_hbm.1) | copy-start | bytes 2359300
  2.9 1.1 %copy-start.2 = (s32[8,96,256]{2,1,0:T(8,128)S(1)}, s32[8,96,256]{2,1,0:T(8,128)}, u32[]{:S(2)}) copy-start(s32[8,96,256]{2,1,0:T(8,128)} %lit_hbm.1) | copy-start | bytes 2359300
  4.0 0.7 %copy-start.3 = (f32[8]{0:T(128)S(1)}, f32[8]{0:T(128)}, u32[]{:S(2)}) copy-start(f32[8]{0:T(128)} %solid.1) | copy-start | bytes 100

commit v2 on v1

--- a/solution.py
+++ b/solution.py
@@ -50,9 +50,21 @@
     return jnp.where(high, jnp.where(odd, d, c), jnp.where(odd, b, a))
 
 
-def kernel(sizes, p_hbm, por_hbm, lit_hbm, solid, pn_out, phi_out, thick_out,
-           pv, hv, qv, tz, tx, tym, typ, rd, ob, por, lit, col, col_send, above,
-           xs, xr, ys, yr, xqs, xqr, yqs, yqr, load_sem, send_sem, recv_sem):
+def beside_y(value, halo, index, r):
+    ny = value.shape[1]
+    lane = lax.broadcasted_iota(jnp.int32, (ROWS, ny), 1)
+    lo = pltpu.roll(halo[0, pl.ds(r, ROWS), :], lax.rem(128 - index, 128), 1)
+    hi = pltpu.roll(halo[1, pl.ds(r, ROWS), :], 127 - index, 1)
+    wide = lambda v: jnp.concatenate([v] * (ny // 128), axis=1)
+    before = jnp.where(lane == 0, wide(lo), pltpu.roll(value, 1, 1))
+    after = jnp.where(lane == ny - 1, wide(hi), pltpu.roll(value, ny - 1, 1))
+    return before, after
+
+
+def exchange(sizes, p_hbm, por_hbm, lit_hbm, solid_hbm,
+             pv, qv, tz, tx, tym, typ, rd, ob, lit, above, yqr,
+             hv, por, col, col_send, xs, xr, ys, yr, xqs, xqr, yqs,
+             solid, load_sem, send_sem, recv_sem):
     nz, nx, ny = por.shape
     axes = ("slab", "mapx", "mapy")
     me = {a: lax.axis_index(a) for a in axes}
@@ -65,6 +77,7 @@
         pltpu.make_async_copy(por_hbm, por, load_sem.at[0]),
         pltpu.make_async_copy(lit_hbm, lit, load_sem.at[1]),
         pltpu.make_async_copy(p_hbm, pv.at[pl.ds(1, nz), inner, :], load_sem.at[2]),
+        pltpu.make_async_copy(solid_hbm, solid, load_sem.at[3]),
     ]
     for c in loads:
         c.start()
@@ -192,6 +205,7 @@
     face_y((pv, hv), ys)
     start(Y_1)
 
+    loads[3].wait()
     for r in range(0, nx, 32):
         rows = pl.ds(r, 32)
 
@@ -231,16 +245,6 @@
     arrived(Y_1)
     arrived(Z_P)
     arrived(Z_H)
-
-    lane = lax.broadcasted_iota(jnp.int32, (ROWS, ny), 1)
-
-    def beside_y(value, halo, index, r):
-        lo = pltpu.roll(halo[0, pl.ds(r, ROWS), :], lax.rem(128 - index, 128), 1)
-        hi = pltpu.roll(halo[1, pl.ds(r, ROWS), :], 127 - index, 1)
-        wide = lambda v: jnp.concatenate([v] * (ny // 128), axis=1)
-        before = jnp.where(lane == 0, wide(lo), pltpu.roll(value, 1, 1))
-        after = jnp.where(lane == ny - 1, wide(hi), pltpu.roll(value, ny - 1, 1))
-        return before, after
 
     def first(z):
         for r in range(0, nx, ROWS):
@@ -289,6 +293,25 @@
     arrived(Y_Q)
     arrived(Z_Q)
 
+    for group in groups:
+        sent(group)
+
+    @pl.when(has_hi["slab"])
+    def _():
+        chain(col_send).wait_send()
+
+
+def finish(pv, qv, tz, tx, tym, typ, rd, ob, lit, above, yqr, solid_hbm,
+           pn_out, phi_out, thick_out, buf, solid, load_sem, store_sem):
+    nz, nx, ny = lit.shape
+    load = pltpu.make_async_copy(solid_hbm, solid, load_sem)
+    load.start()
+    load.wait()
+    outs = (pn_out, phi_out, thick_out)
+
+    def store(i, z):
+        return pltpu.make_async_copy(buf.at[i, z], outs[i].at[z], store_sem.at[i, z])
+
     def second(z, carry):
         for r in range(0, nx, ROWS):
             at = lambda ref, dz, dx: ref[z + 1 + dz, pl.ds(PAD + r + dx, ROWS), :]
@@ -302,51 +325,69 @@
             stress = jnp.maximum(above[rows, :] + ob[z, rows, :] - pn, 0.0)
             cls = classes(lit[z, rows, :])
             phi = pick(cls, PHI_SURFACE) * jnp.exp(pick(cls, ATHY_NEG) * stress)
-            pn_out[z, rows, :] = pn
-            phi_out[z, rows, :] = phi
-            thick_out[z, rows, :] = solid[z] * rec(1.0 - phi)
+            buf[0, z, rows, :] = pn
+            buf[1, z, rows, :] = phi
+            buf[2, z, rows, :] = solid[z] * rec(1.0 - phi)
+        for i in range(3):
+            store(i, z).start()
         return carry
 
     lax.fori_loop(0, nz, second, 0)
 
-    for group in groups:
-        sent(group)
-
-    @pl.when(has_hi["slab"])
-    def _():
-        chain(col_send).wait_send()
+    def stored(z, carry):
+        for i in range(3):
+            store(i, z).wait()
+        return carry
+
+    lax.fori_loop(0, nz, stored, 0)
 
 
 def body(sizes, pressure, porosity, lithology, layer_solid):
     nz, nx, ny = pressure.shape
-    f32 = jnp.float32
-    block = pltpu.VMEM((nz, nx, ny), f32)
-    padded = pltpu.VMEM((nz + 2, nx + 2 * PAD, ny), f32)
-    plane = pltpu.VMEM((nx, ny), f32)
-    out = jax.ShapeDtypeStruct((nz, nx, ny), f32)
+    f32, i32 = jnp.float32, jnp.int32
+    shaped = jax.ShapeDtypeStruct
+    block, plane = (nz, nx, ny), (nx, ny)
+    padded = (nz + 2, nx + 2 * PAD, ny)
+    x_face, y_face = (2, nz, ny), (2, nx, 128)
     vmem = pl.BlockSpec(memory_space=pltpu.VMEM)
-    return pl.pallas_call(
-        functools.partial(kernel, sizes),
-        out_shape=(out, out, out),
-        in_specs=[pl.BlockSpec(memory_space=pl.ANY)] * 3 + [pl.BlockSpec(memory_space=pltpu.SMEM)],
-        out_specs=(vmem, vmem, vmem),
+    hbm = pl.BlockSpec(memory_space=pltpu.HBM)
+    held = [padded, padded, (nz + 1, nx, ny), (nz, nx + PAD, ny), block, block, block, block]
+    held = [shaped(s, f32) for s in held]
+    held += [shaped(block, i32), shaped(plane, f32), shaped(y_face, f32)]
+    held = pl.pallas_call(
+        functools.partial(exchange, sizes),
+        out_shape=tuple(held),
+        in_specs=[hbm] * 4,
+        out_specs=(vmem,) * len(held),
         scratch_shapes=[
-            padded, padded, padded,
-            pltpu.VMEM((nz + 1, nx, ny), f32), pltpu.VMEM((nz, nx + PAD, ny), f32),
-            block, block, block, block, block, pltpu.VMEM((nz, nx, ny), jnp.int32),
-            plane, plane, plane,
+            pltpu.VMEM(padded, f32), pltpu.VMEM(block, f32), pltpu.VMEM(plane, f32),
+            pltpu.VMEM(plane, f32),
             pltpu.VMEM((2, 2 * nz, ny), f32), pltpu.VMEM((2, 2 * nz, ny), f32),
-            pltpu.VMEM((2, nx, 128), f32), pltpu.VMEM((2, nx, 128), f32),
-            pltpu.VMEM((2, nz, ny), f32), pltpu.VMEM((2, nz, ny), f32),
-            pltpu.VMEM((2, nx, 128), f32), pltpu.VMEM((2, nx, 128), f32),
-            pltpu.SemaphoreType.DMA((3,)),
+            pltpu.VMEM(y_face, f32), pltpu.VMEM(y_face, f32),
+            pltpu.VMEM(x_face, f32), pltpu.VMEM(x_face, f32), pltpu.VMEM(y_face, f32),
+            pltpu.SMEM((nz,), f32),
+            pltpu.SemaphoreType.DMA((4,)),
             pltpu.SemaphoreType.DMA((MESSAGES,)),
             pltpu.SemaphoreType.DMA((MESSAGES,)),
         ],
         compiler_params=pltpu.CompilerParams(
-            collective_id=0, has_side_effects=True, vmem_limit_bytes=32 * 2**20),
-        name="basin",
-    )(pressure, porosity, lithology, layer_solid)
+            collective_id=0, has_side_effects=True, vmem_limit_bytes=24 * 2**20),
+        name="exchange",
+    )(*(pltpu.with_memory_space_constraint(a, pltpu.HBM) for a in (pressure, porosity, lithology, layer_solid)))
+    return pl.pallas_call(
+        finish,
+        out_shape=(shaped(block, f32),) * 3,
+        in_specs=[vmem] * len(held) + [hbm],
+        out_specs=(hbm,) * 3,
+        scratch_shapes=[
+            pltpu.VMEM((3,) + block, f32),
+            pltpu.SMEM((nz,), f32),
+            pltpu.SemaphoreType.DMA,
+            pltpu.SemaphoreType.DMA((3, nz)),
+        ],
+        compiler_params=pltpu.CompilerParams(vmem_limit_bytes=24 * 2**20),
+        name="finish",
+    )(*held, layer_solid)
 
 
 def solution(mesh):

time: 23.1 us -> 17.4 us (0.75)
  local copies, waits for them, and re-layouts: 6.69 us -> 0.01 us
  Pallas kernels: 15.6 us -> 16.6 us
    unnamed x11 -> x2, local copies, waits for them, and re-layouts: 6.69 us -> 0.01 us
    pallas_call x1 -> x2, Pallas kernels: 15.6 us -> 16.6 us  [the longest x1 13.2 us: body(): pl.pallas_call(functools.partial(exchange, sizes), out_shape=tuple(held),...]
where the time goes in v2:
time: 17.4 us; the launch traced here: 17.2 us
  Pallas kernels  16.6 us (95%)
  between operations  0.65 us (4%)
    pallas_call x1, Pallas kernels, body(): pl.pallas_call(functools.partial(exchange, sizes), out_shape=tuple(held),...  13.2 us
    pallas_call x1, Pallas kernels, body(): pl.pallas_call(finish, out_shape=(shaped(block, f32),) * 3, in_specs=[vme...  3.41 us

profile of v2, /device:TPU:0, one launch (start us, length us, event | category | flops | bytes accessed | tf_op | source)
XLA Modules:
  0.0 17.2 jit_solution(7863877519008198124)
XLA Ops:
  0.6 0.0 copy-start
  0.6 13.2 %exchange.1 = (f32[10,112,256]{2,1,0:T(8,128)S(1)}, f32[10,112,256]{2,1,0:T(8,128)S(1)}, f32[9,96,256]{2,1,0:T(8,128)S(1)}, f32[8,104,256]{2,1,0:T(8,128)S(1)}, ...) custom-call(f32[8,96,256]{2,1,0:T(8,128)} %p_hbm.1, ...), custom_call_target="tpu_custom_call" | custom-call | tf_op jit(solution)/shard_map/exchange/pallas_call | solution.py:357
  13.8 0.0 copy-done
  13.8 3.4 %finish.1 = (f32[8,96,256]{2,1,0:T(8,128)}, f32[8,96,256]{2,1,0:T(8,128)}, f32[8,96,256]{2,1,0:T(8,128)}) custom-call(f32[10,112,256]{2,1,0:T(8,128)S(1)} %get-tuple-element.14.pv, f32[10,112,256]{2,1,0:T(8,128)S(1)} %get-tuple-element.15.qv, f32[9,96,256]{2,1,0:T(8,128)S(1)} %get-tuple-element.16.tz, f32[8,104,256]{2,1,0:T(8,128)S(1)} %get-tuple-element.17.tx, ...), custom_call_target="tpu_custom_call" | custom-call | tf_op jit(solution)/shard_map/finish/pallas_call | solution.py:377
Async XLA Ops:
  0.6 13.2 %copy-start = (f32[8]{0:T(128)S(1)}, f32[8]{0:T(128)}, u32[]{:S(2)}) copy-start(f32[8]{0:T(128)} %solid_hbm.3) | copy-start | bytes 100

commit v3 on v2

--- a/solution.py
+++ b/solution.py
@@ -36,8 +36,7 @@
 
 
 def rec(x):
-    r = pl.reciprocal(x, approx=True)
-    return r * (2.0 - x * r)
+    return pl.reciprocal(x, approx=True)
 
 
 def classes(lith):
@@ -62,9 +61,9 @@
 
 
 def exchange(sizes, p_hbm, por_hbm, lit_hbm, solid_hbm,
-             pv, qv, tz, tx, tym, typ, rd, ob, lit, above, yqr,
-             hv, por, col, col_send, xs, xr, ys, yr, xqs, xqr, yqs,
-             solid, load_sem, send_sem, recv_sem):
+             part, ob, lit, above, y_term, solid_wide,
+             pv, qv, hv, tz, tx, tym, typ, rd, por, col, col_send, xs, xr, ys, yr,
+             zqr, xqs, xqr, yqs, yqr, edge, solid, load_sem, send_sem, recv_sem):
     nz, nx, ny = por.shape
     axes = ("slab", "mapx", "mapy")
     me = {a: lax.axis_index(a) for a in axes}
@@ -109,8 +108,7 @@
                   hv.at[1, inner, :], hv.at[z_hi, inner, :]),
         X_1: pair(X_1, "mapx", xs.at[0], xr.at[0], xs.at[1], xr.at[1]),
         Y_1: pair(Y_1, "mapy", ys.at[0], yr.at[0], ys.at[1], yr.at[1]),
-        Z_Q: pair(Z_Q, "slab", qv.at[nz, inner, :], qv.at[z_lo, inner, :],
-                  qv.at[1, inner, :], qv.at[z_hi, inner, :]),
+        Z_Q: pair(Z_Q, "slab", qv.at[nz, inner, :], zqr.at[0], qv.at[1, inner, :], zqr.at[1]),
         X_Q: pair(X_Q, "mapx", xqs.at[0], xqr.at[0], xqs.at[1], xqr.at[1]),
         Y_Q: pair(Y_Q, "mapy", yqs.at[0], yqr.at[0], yqs.at[1], yqr.at[1]),
     }
@@ -135,6 +133,12 @@
 
     lane_y = lax.broadcasted_iota(jnp.int32, (nx, 128), 1)
 
+    for layer in (z_lo, z_hi):
+        qv[layer, inner, :] = jnp.zeros((nx, ny), jnp.float32)
+    for z in range(nz):
+        for row in (PAD - 1, PAD + nx):
+            qv[z + 1, pl.ds(row, 1), :] = jnp.zeros((1, ny), jnp.float32)
+
     for axis, flags in (("lo", has_lo), ("hi", has_hi)):
         side = 0 if axis == "lo" else 1
         layer = z_lo if side == 0 else z_hi
@@ -142,7 +146,7 @@
         @pl.when(jnp.logical_not(flags["slab"]))
         def _():
             pv[layer, inner, :] = jnp.zeros((nx, ny), jnp.float32)
-            qv[layer, inner, :] = jnp.zeros((nx, ny), jnp.float32)
+            zqr[side] = jnp.zeros((nx, ny), jnp.float32)
             hv[layer, inner, :] = jnp.full((nx, ny), OUTSIDE, jnp.float32)
             if side == 0:
                 above[...] = jnp.zeros((nx, ny), jnp.float32)
@@ -158,9 +162,6 @@
             yr[side] = jnp.where(lane_y < nz, jnp.float32(0.0), jnp.float32(OUTSIDE))
             yqr[side] = jnp.zeros((nx, 128), jnp.float32)
 
-    pl.semaphore_wait(barrier, peers)
-
-    start(Z_P)
     loads[0].wait()
     loads[1].wait()
 
@@ -173,7 +174,9 @@
 
     half_inverse(0)
     half_inverse(nz - 1)
+    pl.semaphore_wait(barrier, peers)
     start(Z_H)
+    start(Z_P)
     lax.fori_loop(1, nz - 1, lambda z, c: (half_inverse(z), c)[1], 0)
     loads[2].wait()
 
@@ -246,14 +249,15 @@
     arrived(Z_P)
     arrived(Z_H)
 
-    def first(z):
+    def first(z, below_known=True):
         for r in range(0, nx, ROWS):
             at = lambda ref, dz, dx: ref[z + 1 + dz, pl.ds(PAD + r + dx, ROWS), :]
             rows = pl.ds(r, ROWS)
             h, p = at(hv, 0, 0), at(pv, 0, 0)
             h_before, h_after = beside_y(h, yr, nz + z, r)
             p_before, p_after = beside_y(p, yr, z, r)
-            t_zm, t_zp = rec(h + at(hv, -1, 0)), rec(h + at(hv, 1, 0))
+            t_zm = tz[z, rows, :] if below_known else rec(h + at(hv, -1, 0))
+            t_zp = rec(h + at(hv, 1, 0))
             t_xm, t_xp = rec(h + at(hv, 0, -1)), rec(h + at(hv, 0, 1))
             t_ym, t_yp = rec(h + h_before), rec(h + h_after)
             diag = 1.0 + ((t_zm + t_zp) + (t_xm + t_xp) + (t_ym + t_yp))
@@ -261,18 +265,19 @@
             total = (p + (t_zm * at(pv, -1, 0) + t_zp * at(pv, 1, 0))
                      + (t_xm * at(pv, 0, -1) + t_xp * at(pv, 0, 1))
                      + (t_ym * p_before + t_yp * p_after))
-            tz[z, rows, :] = t_zm
+            if not below_known:
+                tz[z, rows, :] = t_zm
             tz[z + 1, rows, :] = t_zp
             tx[z, rows, :] = t_xm
             if r + ROWS == nx:
                 tx[z, pl.ds(nx, 1), :] = t_xp[ROWS - 1:, :]
             tym[z, rows, :] = t_ym
             typ[z, rows, :] = t_yp
-            rd[z, rows, :] = inv
+            rd[z, rows, :] = STEP_RES * inv
             qv[z + 1, pl.ds(PAD + r, ROWS), :] = total * inv
 
-    first(0)
-    first(nz - 1)
+    first(0, False)
+    first(nz - 1, False)
     start(Z_Q)
     lax.fori_loop(1, nz - 1, lambda z, c: (first(z), c)[1], 0)
     face_x(qv, xqs, 0)
@@ -280,59 +285,99 @@
     face_y((qv,), yqs)
     start(Y_Q)
 
+    for side in range(2):
+        for r in range(0, nx, 32):
+            rows, lane = pl.ds(r, 32), lane_y[:32]
+            acc = jnp.zeros((32, 128), jnp.float32)
+            for z in range(nz):
+                if side == 0:
+                    term = tym[z, rows, pl.ds(0, 128)] * rd[z, rows, pl.ds(0, 128)]
+                    moved = pltpu.roll(term, z, 1) if z else term
+                else:
+                    lanes = pl.ds(ny - 128, 128)
+                    term = typ[z, rows, lanes] * rd[z, rows, lanes]
+                    moved = pltpu.roll(term, z + 1, 1)
+                acc = jnp.where(lane == z, moved, acc)
+            edge[side, rows, :] = acc
+
     @pl.when(me["slab"] == 2)
     def _():
         forward()
 
-    @pl.when(me["slab"] == 3)
-    def _():
-        chain(col_send).wait_recv()
-
-    arrived(X_Q)
-    spread_x(xqr, 0, qv)
-    arrived(Y_Q)
-    arrived(Z_Q)
-
-    for group in groups:
-        sent(group)
-
-    @pl.when(has_hi["slab"])
-    def _():
-        chain(col_send).wait_send()
-
-
-def finish(pv, qv, tz, tx, tym, typ, rd, ob, lit, above, yqr, solid_hbm,
-           pn_out, phi_out, thick_out, buf, solid, load_sem, store_sem):
-    nz, nx, ny = lit.shape
-    load = pltpu.make_async_copy(solid_hbm, solid, load_sem)
-    load.start()
-    load.wait()
-    outs = (pn_out, phi_out, thick_out)
-
-    def store(i, z):
-        return pltpu.make_async_copy(buf.at[i, z], outs[i].at[z], store_sem.at[i, z])
+    lane = lax.broadcasted_iota(jnp.int32, (ROWS, ny), 1)
 
     def second(z, carry):
         for r in range(0, nx, ROWS):
             at = lambda ref, dz, dx: ref[z + 1 + dz, pl.ds(PAD + r + dx, ROWS), :]
             rows = pl.ds(r, ROWS)
             p, q = at(pv, 0, 0), at(qv, 0, 0)
-            q_before, q_after = beside_y(q, yqr, z, r)
+            q_before = jnp.where(lane == 0, 0.0, pltpu.roll(q, 1, 1))
+            q_after = jnp.where(lane == ny - 1, 0.0, pltpu.roll(q, ny - 1, 1))
             total = (p + (tz[z, rows, :] * at(qv, -1, 0) + tz[z + 1, rows, :] * at(qv, 1, 0))
                      + (tx[z, rows, :] * at(qv, 0, -1) + tx[z, pl.ds(r + 1, ROWS), :] * at(qv, 0, 1))
                      + (tym[z, rows, :] * q_before + typ[z, rows, :] * q_after))
-            pn = q + STEP_KEEP * (q - p) + STEP_RES * (total * rd[z, rows, :] - q)
+            part[z, rows, :] = q + STEP_KEEP * (q - p) + (total * rd[z, rows, :] - STEP_RES * q)
+        return carry
+
+    lax.fori_loop(0, nz, second, 0)
+
+    arrived(X_Q)
+    for side, row in ((0, 0), (1, nx - 1)):
+        for z in range(nz):
+            one = pl.ds(row, 1)
+            part[z, one, :] += rd[z, one, :] * tx[z, pl.ds(row + side, 1), :] * xqr[side, pl.ds(z, 1), :]
+    arrived(Y_Q)
+    for side in range(2):
+        y_term[side] = edge[side] * yqr[side]
+    arrived(Z_Q)
+    for side, z in ((0, 0), (1, nz - 1)):
+        for r in range(0, nx, 32):
+            rows = pl.ds(r, 32)
+            part[z, rows, :] += rd[z, rows, :] * tz[z + side, rows, :] * zqr[side, rows, :]
+    for z in range(nz):
+        solid_wide[z] = jnp.full((8, 128), solid[z], jnp.float32)
+
+    @pl.when(me["slab"] == 3)
+    def _():
+        chain(col_send).wait_recv()
+
+    for group in groups:
+        sent(group)
+
+    @pl.when(has_hi["slab"])
+    def _():
+        chain(col_send).wait_send()
+
+
+def finish(part, ob, lit, above, y_term, solid_wide, pn_out, phi_out, thick_out, buf, store_sem):
+    nz, nx, ny = lit.shape
+    outs = (pn_out, phi_out, thick_out)
+    lane = lax.broadcasted_iota(jnp.int32, (ROWS, 128), 1)
+
+    def store(i, z):
+        return pltpu.make_async_copy(buf.at[i, z], outs[i].at[z], store_sem.at[i, z])
+
+    def layer(z, carry):
+        solid = jnp.concatenate([solid_wide[z]] * (ny // 128), axis=1)
+        solid = jnp.concatenate([solid] * (ROWS // 8), axis=0)
+        for r in range(0, nx, ROWS):
+            rows = pl.ds(r, ROWS)
+            lo = pltpu.roll(y_term[0, rows, :], lax.rem(128 - z, 128), 1)
+            hi = pltpu.roll(y_term[1, rows, :], 127 - z, 1)
+            lo, hi = jnp.where(lane == 0, lo, 0.0), jnp.where(lane == 127, hi, 0.0)
+            zeros = [jnp.zeros((ROWS, 128), jnp.float32)] * (ny // 128 - 2)
+            pn = part[z, rows, :] + jnp.concatenate([lo] + zeros + [hi], axis=1)
             stress = jnp.maximum(above[rows, :] + ob[z, rows, :] - pn, 0.0)
             cls = classes(lit[z, rows, :])
             phi = pick(cls, PHI_SURFACE) * jnp.exp(pick(cls, ATHY_NEG) * stress)
             buf[0, z, rows, :] = pn
             buf[1, z, rows, :] = phi
-            buf[2, z, rows, :] = solid[z] * rec(1.0 - phi)
+            buf[2, z, rows, :] = solid * rec(1.0 - phi)
         for i in range(3):
             store(i, z).start()
         return carry
 
-    lax.fori_loop(0, nz, second, 0)
+    lax.fori_loop(0, nz, layer, 0)
 
     def stored(z, carry):
         for i in range(3):
@@ -351,20 +396,18 @@
     x_face, y_face = (2, nz, ny), (2, nx, 128)
     vmem = pl.BlockSpec(memory_space=pltpu.VMEM)
     hbm = pl.BlockSpec(memory_space=pltpu.HBM)
-    held = [padded, padded, (nz + 1, nx, ny), (nz, nx + PAD, ny), block, block, block, block]
-    held = [shaped(s, f32) for s in held]
-    held += [shaped(block, i32), shaped(plane, f32), shaped(y_face, f32)]
+    held = (shaped(block, f32), shaped(block, f32), shaped(block, i32), shaped(plane, f32),
+            shaped(y_face, f32), shaped((nz, 8, 128), f32))
     held = pl.pallas_call(
         functools.partial(exchange, sizes),
-        out_shape=tuple(held),
+        out_shape=held,
         in_specs=[hbm] * 4,
         out_specs=(vmem,) * len(held),
-        scratch_shapes=[
-            pltpu.VMEM(padded, f32), pltpu.VMEM(block, f32), pltpu.VMEM(plane, f32),
-            pltpu.VMEM(plane, f32),
-            pltpu.VMEM((2, 2 * nz, ny), f32), pltpu.VMEM((2, 2 * nz, ny), f32),
-            pltpu.VMEM(y_face, f32), pltpu.VMEM(y_face, f32),
-            pltpu.VMEM(x_face, f32), pltpu.VMEM(x_face, f32), pltpu.VMEM(y_face, f32),
+        scratch_shapes=[pltpu.VMEM(shape, f32) for shape in (
+            padded, padded, padded, (nz + 1, nx, ny), (nz, nx + PAD, ny),
+            block, block, block, block, plane, plane,
+            (2, 2 * nz, ny), (2, 2 * nz, ny), y_face, y_face,
+            (2, nx, ny), x_face, x_face, y_face, y_face, y_face)] + [
             pltpu.SMEM((nz,), f32),
             pltpu.SemaphoreType.DMA((4,)),
             pltpu.SemaphoreType.DMA((MESSAGES,)),
@@ -377,17 +420,15 @@
     return pl.pallas_call(
         finish,
         out_shape=(shaped(block, f32),) * 3,
-        in_specs=[vmem] * len(held) + [hbm],
+        in_specs=[vmem] * len(held),
         out_specs=(hbm,) * 3,
         scratch_shapes=[
             pltpu.VMEM((3,) + block, f32),
-            pltpu.SMEM((nz,), f32),
-            pltpu.SemaphoreType.DMA,
             pltpu.SemaphoreType.DMA((3, nz)),
         ],
         compiler_params=pltpu.CompilerParams(vmem_limit_bytes=24 * 2**20),
         name="finish",
-    )(*held, layer_solid)
+    )(*held)
 
 
 def solution(mesh):

time: 17.4 us -> 15.5 us (0.89)
  Pallas kernels: 16.6 us -> 14.7 us
    pallas_call x1, Pallas kernels: 3.41 us -> 1.94 us  [body(): pl.pallas_call(finish, out_shape=(shaped(block, f32),) * 3, in_specs=[vme...]
    pallas_call x1, Pallas kernels: 13.2 us -> 12.8 us  [body(): pl.pallas_call(functools.partial(exchange, sizes), out_shape=held, in_spe...]
where the time goes in v3:
time: 15.5 us; the launch traced here: 15.4 us
  Pallas kernels  14.7 us (95%)
  between operations  0.64 us (4%)
    pallas_call x1, Pallas kernels, body(): pl.pallas_call(functools.partial(exchange, sizes), out_shape=held, in_spe...  12.8 us
    pallas_call x1, Pallas kernels, body(): pl.pallas_call(finish, out_shape=(shaped(block, f32),) * 3, in_specs=[vme...  1.94 us

profile of v3, /device:TPU:0, one launch (start us, length us, event | category | flops | bytes accessed | tf_op | source)
XLA Modules:
  0.0 15.4 jit_solution(5616954548155013212)
XLA Ops:
  0.6 12.8 %exchange.1 = (f32[8,96,256]{2,1,0:T(8,128)S(1)}, f32[8,96,256]{2,1,0:T(8,128)S(1)}, s32[8,96,256]{2,1,0:T(8,128)S(1)}, f32[96,256]{1,0:T(8,128)S(1)}, f32[2,96,...) custom-call(f32[8,96,256]{2,1,0:T(8,128)} %p_hbm.1, f32[8,96,256]{2,1,0:T(8,128)} %por_hbm.1, s32[8,96,256]{2,1,0:T(8,128)} %lit_hbm.1, ...), custom_call_target="tpu_custom_call" | custom-call | tf_op jit(solution)/shard_map/exchange/pallas_call | solution.py:401
  13.5 1.9 %finish.1 = (f32[8,96,256]{2,1,0:T(8,128)}, f32[8,96,256]{2,1,0:T(8,128)}, f32[8,96,256]{2,1,0:T(8,128)}) custom-call(f32[8,96,256]{2,1,0:T(8,128)S(1)} %get-tuple-element.9.part, f32[8,96,256]{2,1,0:T(8,128)S(1)} %get-tuple-element.10.ob, s32[8,96,256]{2,1,0:T(8,128)S(1)} %get-tuple-element.11.lit, f32[96,256]{1,0:T(8,128)S(1)} %get-tuple-element.12.above, ...), custom_call_target="tpu_custom_call" | custom-call | tf_op jit(solution)/shard_map/finish/pallas_call | solution.py:420

commit v4 on v3

--- a/solution.py
+++ b/solution.py
@@ -22,10 +22,12 @@
 STEP_KEEP = RHO_SECOND * RHO_FIRST
 STEP_RES = 2.0 * RHO_SECOND / SPECTRUM_HALF
 
-HALF_BASE = tuple(-(b - 0.35 * s) - math.log(2.0) for b, s in zip(MOB_BASE, MOB_SLOPE))
-HALF_SLOPE = tuple(-s for s in MOB_SLOPE)
+LOG2_E = 1.0 / math.log(2.0)
+
+HALF_BASE = tuple(-(b - 0.35 * s) * LOG2_E - 1.0 for b, s in zip(MOB_BASE, MOB_SLOPE))
+HALF_SLOPE = tuple(-s * LOG2_E for s in MOB_SLOPE)
 GRAIN_LESS = tuple(g - WATER_DENSITY for g in GRAIN_DENSITY)
-ATHY_NEG = tuple(-a for a in ATHY_RATE)
+ATHY_NEG = tuple(-a * LOG2_E for a in ATHY_RATE)
 OUTSIDE = 2.0e38
 
 MESH = pl.DeviceIdType.MESH
@@ -49,15 +51,21 @@
     return jnp.where(high, jnp.where(odd, d, c), jnp.where(odd, b, a))
 
 
-def beside_y(value, halo, index, r):
-    ny = value.shape[1]
-    lane = lax.broadcasted_iota(jnp.int32, (ROWS, ny), 1)
-    lo = pltpu.roll(halo[0, pl.ds(r, ROWS), :], lax.rem(128 - index, 128), 1)
-    hi = pltpu.roll(halo[1, pl.ds(r, ROWS), :], 127 - index, 1)
-    wide = lambda v: jnp.concatenate([v] * (ny // 128), axis=1)
-    before = jnp.where(lane == 0, wide(lo), pltpu.roll(value, 1, 1))
-    after = jnp.where(lane == ny - 1, wide(hi), pltpu.roll(value, ny - 1, 1))
-    return before, after
+def beside_y(value, lo, hi):
+    rows, ny = value.shape
+    lane = lax.broadcasted_iota(jnp.int32, (rows, 128), 1)
+    parts = [value[:, y:y + 128] for y in range(0, ny, 128)]
+    later = [pltpu.roll(v, 1, 1) for v in parts]
+    earlier = [pltpu.roll(v, 127, 1) for v in parts]
+    before = [jnp.where(lane == 0, a, b) for a, b in zip([lo] + later[:-1], later)]
+    after = [jnp.where(lane == 127, a, b) for a, b in zip(earlier[1:] + [hi], earlier)]
+    return jnp.concatenate(before, axis=1), jnp.concatenate(after, axis=1)
+
+
+def unpacked(halo, index, rows):
+    lo = pltpu.roll(halo[0, rows, :], lax.rem(128 - index, 128), 1)
+    hi = pltpu.roll(halo[1, rows, :], 127 - index, 1)
+    return lo, hi
 
 
 def exchange(sizes, p_hbm, por_hbm, lit_hbm, solid_hbm,
@@ -169,7 +177,7 @@
         for r in range(0, nx, 32):
             rows = pl.ds(r, 32)
             cls = classes(lit[z, rows, :])
-            hv[z + 1, pl.ds(PAD + r, 32), :] = jnp.exp(
+            hv[z + 1, pl.ds(PAD + r, 32), :] = jnp.exp2(
                 pick(cls, HALF_BASE) + pick(cls, HALF_SLOPE) * por[z, rows, :])
 
     half_inverse(0)
@@ -233,10 +241,6 @@
         col_send[...] = col[...] + above[...]
         chain(col_send).start()
 
-    @pl.when(me["slab"] == 1)
-    def _():
-        forward()
-
     def spread_x(src, offset, dst):
         for side, row in ((0, PAD - 1), (1, PAD + nx)):
             for z in range(nz):
@@ -246,18 +250,16 @@
     spread_x(xr, 0, pv)
     spread_x(xr, nz, hv)
     arrived(Y_1)
-    arrived(Z_P)
-    arrived(Z_H)
-
-    def first(z, below_known=True):
+
+    def first(z, below=True, above_known=False):
         for r in range(0, nx, ROWS):
             at = lambda ref, dz, dx: ref[z + 1 + dz, pl.ds(PAD + r + dx, ROWS), :]
             rows = pl.ds(r, ROWS)
             h, p = at(hv, 0, 0), at(pv, 0, 0)
-            h_before, h_after = beside_y(h, yr, nz + z, r)
-            p_before, p_after = beside_y(p, yr, z, r)
-            t_zm = tz[z, rows, :] if below_known else rec(h + at(hv, -1, 0))
-            t_zp = rec(h + at(hv, 1, 0))
+            h_before, h_after = beside_y(h, *unpacked(yr, nz + z, rows))
+            p_before, p_after = beside_y(p, *unpacked(yr, z, rows))
+            t_zm = tz[z, rows, :] if below else rec(h + at(hv, -1, 0))
+            t_zp = tz[z + 1, rows, :] if above_known else rec(h + at(hv, 1, 0))
             t_xm, t_xp = rec(h + at(hv, 0, -1)), rec(h + at(hv, 0, 1))
             t_ym, t_yp = rec(h + h_before), rec(h + h_after)
             diag = 1.0 + ((t_zm + t_zp) + (t_xm + t_xp) + (t_ym + t_yp))
@@ -265,9 +267,10 @@
             total = (p + (t_zm * at(pv, -1, 0) + t_zp * at(pv, 1, 0))
                      + (t_xm * at(pv, 0, -1) + t_xp * at(pv, 0, 1))
                      + (t_ym * p_before + t_yp * p_after))
-            if not below_known:
+            if not below:
                 tz[z, rows, :] = t_zm
-            tz[z + 1, rows, :] = t_zp
+            if not above_known:
+                tz[z + 1, rows, :] = t_zp
             tx[z, rows, :] = t_xm
             if r + ROWS == nx:
                 tx[z, pl.ds(nx, 1), :] = t_xp[ROWS - 1:, :]
@@ -276,10 +279,19 @@
             rd[z, rows, :] = STEP_RES * inv
             qv[z + 1, pl.ds(PAD + r, ROWS), :] = total * inv
 
-    first(0, False)
-    first(nz - 1, False)
+    first(1, below=False)
+    lax.fori_loop(2, nz // 2, lambda z, c: (first(z), c)[1], 0)
+
+    @pl.when(me["slab"] == 1)
+    def _():
+        forward()
+
+    lax.fori_loop(nz // 2, nz - 1, lambda z, c: (first(z), c)[1], 0)
+    arrived(Z_H)
+    arrived(Z_P)
+    first(0, below=False, above_known=True)
+    first(nz - 1)
     start(Z_Q)
-    lax.fori_loop(1, nz - 1, lambda z, c: (first(z), c)[1], 0)
     face_x(qv, xqs, 0)
     start(X_Q)
     face_y((qv,), yqs)
@@ -304,15 +316,12 @@
     def _():
         forward()
 
-    lane = lax.broadcasted_iota(jnp.int32, (ROWS, ny), 1)
-
     def second(z, carry):
         for r in range(0, nx, ROWS):
             at = lambda ref, dz, dx: ref[z + 1 + dz, pl.ds(PAD + r + dx, ROWS), :]
             rows = pl.ds(r, ROWS)
             p, q = at(pv, 0, 0), at(qv, 0, 0)
-            q_before = jnp.where(lane == 0, 0.0, pltpu.roll(q, 1, 1))
-            q_after = jnp.where(lane == ny - 1, 0.0, pltpu.roll(q, ny - 1, 1))
+            q_before, q_after = beside_y(q, 0.0, 0.0)
             total = (p + (tz[z, rows, :] * at(qv, -1, 0) + tz[z + 1, rows, :] * at(qv, 1, 0))
                      + (tx[z, rows, :] * at(qv, 0, -1) + tx[z, pl.ds(r + 1, ROWS), :] * at(qv, 0, 1))
                      + (tym[z, rows, :] * q_before + typ[z, rows, :] * q_after))
@@ -362,14 +371,13 @@
         solid = jnp.concatenate([solid] * (ROWS // 8), axis=0)
         for r in range(0, nx, ROWS):
             rows = pl.ds(r, ROWS)
-            lo = pltpu.roll(y_term[0, rows, :], lax.rem(128 - z, 128), 1)
-            hi = pltpu.roll(y_term[1, rows, :], 127 - z, 1)
+            lo, hi = unpacked(y_term, z, rows)
             lo, hi = jnp.where(lane == 0, lo, 0.0), jnp.where(lane == 127, hi, 0.0)
             zeros = [jnp.zeros((ROWS, 128), jnp.float32)] * (ny // 128 - 2)
             pn = part[z, rows, :] + jnp.concatenate([lo] + zeros + [hi], axis=1)
             stress = jnp.maximum(above[rows, :] + ob[z, rows, :] - pn, 0.0)
             cls = classes(lit[z, rows, :])
-            phi = pick(cls, PHI_SURFACE) * jnp.exp(pick(cls, ATHY_NEG) * stress)
+            phi = pick(cls, PHI_SURFACE) * jnp.exp2(pick(cls, ATHY_NEG) * stress)
             buf[0, z, rows, :] = pn
             buf[1, z, rows, :] = phi
             buf[2, z, rows, :] = solid * rec(1.0 - phi)

time: 15.5 us -> 15.7 us (1.013)
  the two profiles are of different devices: /device:TPU:0 before, /device:TPU:1 now
where the time goes in v4:
time: 15.7 us; the launch traced here: 15.5 us
  Pallas kernels  14.9 us (95%)
  between operations  0.64 us (4%)
    pallas_call x1, Pallas kernels, body(): pl.pallas_call(functools.partial(exchange, sizes), out_shape=held, in_spe...  13 us
    pallas_call x1, Pallas kernels, body(): pl.pallas_call(finish, out_shape=(shaped(block, f32),) * 3, in_specs=[vme...  1.91 us

profile of v4, /device:TPU:1, one launch (start us, length us, event | category | flops | bytes accessed | tf_op | source)
XLA Modules:
  0.0 15.5 jit_solution(15715717695538156711)
XLA Ops:
  0.6 13.0 %exchange.1 = (f32[8,96,256]{2,1,0:T(8,128)S(1)}, f32[8,96,256]{2,1,0:T(8,128)S(1)}, s32[8,96,256]{2,1,0:T(8,128)S(1)}, f32[96,256]{1,0:T(8,128)S(1)}, f32[2,96,...) custom-call(f32[8,96,256]{2,1,0:T(8,128)} %p_hbm.1, f32[8,96,256]{2,1,0:T(8,128)} %por_hbm.1, s32[8,96,256]{2,1,0:T(8,128)} %lit_hbm.1, ...), custom_call_target="tpu_custom_call" | custom-call | tf_op jit(solution)/shard_map/exchange/pallas_call | solution.py:409
  13.6 1.9 %finish.1 = (f32[8,96,256]{2,1,0:T(8,128)}, f32[8,96,256]{2,1,0:T(8,128)}, f32[8,96,256]{2,1,0:T(8,128)}) custom-call(f32[8,96,256]{2,1,0:T(8,128)S(1)} %get-tuple-element.9.part, f32[8,96,256]{2,1,0:T(8,128)S(1)} %get-tuple-element.10.ob, s32[8,96,256]{2,1,0:T(8,128)S(1)} %get-tuple-element.11.lit, f32[96,256]{1,0:T(8,128)S(1)} %get-tuple-element.12.above, ...), custom_call_target="tpu_custom_call" | custom-call | tf_op jit(solution)/shard_map/finish/pallas_call | solution.py:428

commit v5 on v4

--- a/solution.py
+++ b/solution.py
@@ -51,27 +51,31 @@
     return jnp.where(high, jnp.where(odd, d, c), jnp.where(odd, b, a))
 
 
-def beside_y(value, lo, hi):
+def shifted(value, up):
     rows, ny = value.shape
     lane = lax.broadcasted_iota(jnp.int32, (rows, 128), 1)
-    parts = [value[:, y:y + 128] for y in range(0, ny, 128)]
-    later = [pltpu.roll(v, 1, 1) for v in parts]
-    earlier = [pltpu.roll(v, 127, 1) for v in parts]
-    before = [jnp.where(lane == 0, a, b) for a, b in zip([lo] + later[:-1], later)]
-    after = [jnp.where(lane == 127, a, b) for a, b in zip(earlier[1:] + [hi], earlier)]
-    return jnp.concatenate(before, axis=1), jnp.concatenate(after, axis=1)
-
-
-def unpacked(halo, index, rows):
+    parts = [pltpu.roll(value[:, y:y + 128], 1 if up else 127, 1) for y in range(0, ny, 128)]
+    if up:
+        joined = [jnp.where(lane == 0, a, b) for a, b in zip(parts[-1:] + parts[:-1], parts)]
+    else:
+        joined = [jnp.where(lane == 127, a, b) for a, b in zip(parts[1:] + parts[:1], parts)]
+    return jnp.concatenate(joined, axis=1)
+
+
+def at_edges(halo, index, rows, ny):
     lo = pltpu.roll(halo[0, rows, :], lax.rem(128 - index, 128), 1)
     hi = pltpu.roll(halo[1, rows, :], 127 - index, 1)
-    return lo, hi
+    lane = lax.broadcasted_iota(jnp.int32, lo.shape, 1)
+    zeros = [jnp.zeros(lo.shape, jnp.float32)] * (ny // 128 - 2)
+    ends = [jnp.where(lane == 0, lo, 0.0)] + zeros + [jnp.where(lane == 127, hi, 0.0)]
+    return jnp.concatenate(ends, axis=1)
 
 
 def exchange(sizes, p_hbm, por_hbm, lit_hbm, solid_hbm,
              part, ob, lit, above, y_term, solid_wide,
-             pv, qv, hv, tz, tx, tym, typ, rd, por, col, col_send, xs, xr, ys, yr,
-             zqr, xqs, xqr, yqs, yqr, edge, solid, load_sem, send_sem, recv_sem):
+             pv, qv, hv, tz, tx, ty, rd, por, col, col_send, xs, xr, ys, yr,
+             zpr, zhr, zqr, xqs, xqr, yqs, yqr, z_link, x_link, y_link, y_flow, edge,
+             solid, load_sem, send_sem, recv_sem):
     nz, nx, ny = por.shape
     axes = ("slab", "mapx", "mapy")
     me = {a: lax.axis_index(a) for a in axes}
@@ -110,10 +114,8 @@
 
     z_lo, z_hi = 0, nz + 1
     groups = {
-        Z_P: pair(Z_P, "slab", p_hbm.at[nz - 1], pv.at[z_lo, inner, :],
-                  p_hbm.at[0], pv.at[z_hi, inner, :]),
-        Z_H: pair(Z_H, "slab", hv.at[nz, inner, :], hv.at[z_lo, inner, :],
-                  hv.at[1, inner, :], hv.at[z_hi, inner, :]),
+        Z_P: pair(Z_P, "slab", p_hbm.at[nz - 1], zpr.at[0], p_hbm.at[0], zpr.at[1]),
+        Z_H: pair(Z_H, "slab", hv.at[nz, inner, :], zhr.at[0], hv.at[1, inner, :], zhr.at[1]),
         X_1: pair(X_1, "mapx", xs.at[0], xr.at[0], xs.at[1], xr.at[1]),
         Y_1: pair(Y_1, "mapy", ys.at[0], yr.at[0], ys.at[1], yr.at[1]),
         Z_Q: pair(Z_Q, "slab", qv.at[nz, inner, :], zqr.at[0], qv.at[1, inner, :], zqr.at[1]),
@@ -142,20 +144,22 @@
     lane_y = lax.broadcasted_iota(jnp.int32, (nx, 128), 1)
 
     for layer in (z_lo, z_hi):
+        pv[layer, inner, :] = jnp.zeros((nx, ny), jnp.float32)
         qv[layer, inner, :] = jnp.zeros((nx, ny), jnp.float32)
+        hv[layer, inner, :] = jnp.full((nx, ny), OUTSIDE, jnp.float32)
+    tz[0] = jnp.zeros((nx, ny), jnp.float32)
     for z in range(nz):
         for row in (PAD - 1, PAD + nx):
+            pv[z + 1, pl.ds(row, 1), :] = jnp.zeros((1, ny), jnp.float32)
             qv[z + 1, pl.ds(row, 1), :] = jnp.zeros((1, ny), jnp.float32)
-
-    for axis, flags in (("lo", has_lo), ("hi", has_hi)):
-        side = 0 if axis == "lo" else 1
-        layer = z_lo if side == 0 else z_hi
-
+            hv[z + 1, pl.ds(row, 1), :] = jnp.full((1, ny), OUTSIDE, jnp.float32)
+
+    for side, flags in ((0, has_lo), (1, has_hi)):
         @pl.when(jnp.logical_not(flags["slab"]))
         def _():
-            pv[layer, inner, :] = jnp.zeros((nx, ny), jnp.float32)
+            zpr[side] = jnp.zeros((nx, ny), jnp.float32)
             zqr[side] = jnp.zeros((nx, ny), jnp.float32)
-            hv[layer, inner, :] = jnp.full((nx, ny), OUTSIDE, jnp.float32)
+            zhr[side] = jnp.full((nx, ny), OUTSIDE, jnp.float32)
             if side == 0:
                 above[...] = jnp.zeros((nx, ny), jnp.float32)
 
@@ -180,12 +184,7 @@
             hv[z + 1, pl.ds(PAD + r, 32), :] = jnp.exp2(
                 pick(cls, HALF_BASE) + pick(cls, HALF_SLOPE) * por[z, rows, :])
 
-    half_inverse(0)
-    half_inverse(nz - 1)
-    pl.semaphore_wait(barrier, peers)
-    start(Z_H)
-    start(Z_P)
-    lax.fori_loop(1, nz - 1, lambda z, c: (half_inverse(z), c)[1], 0)
+    lax.fori_loop(0, nz, lambda z, c: (half_inverse(z), c)[1], 0)
     loads[2].wait()
 
     def face_x(src, dst, offset):
@@ -193,7 +192,7 @@
             for z in range(nz):
                 dst[side, pl.ds(offset + z, 1), :] = src[z + 1, pl.ds(row, 1), :]
 
-    def face_y(srcs, dst):
+    def face_y(srcs, dst, first_z=1, first_row=PAD):
         for side in range(2):
             for r in range(0, nx, 32):
                 acc = jnp.zeros((32, 128), jnp.float32)
@@ -201,20 +200,19 @@
                 for i, src in enumerate(srcs):
                     for z in range(nz):
                         k = i * nz + z
-                        if side == 0:
-                            col_ = src[z + 1, pl.ds(PAD + r, 32), pl.ds(ny - 128, 128)]
-                            moved = pltpu.roll(col_, k + 1, 1)
-                        else:
-                            col_ = src[z + 1, pl.ds(PAD + r, 32), pl.ds(0, 128)]
-                            moved = pltpu.roll(col_, k, 1) if k else col_
+                        lanes = pl.ds(0 if side else ny - 128, 128)
+                        column = src[z + first_z, pl.ds(first_row + r, 32), lanes]
+                        shift = k if side else k + 1
+                        moved = pltpu.roll(column, shift, 1) if shift else column
                         acc = jnp.where(lane == k, moved, acc)
                 dst[side, pl.ds(r, 32), :] = acc
 
     face_x(pv, xs, 0)
     face_x(hv, xs, nz)
-    start(X_1)
     face_y((pv, hv), ys)
-    start(Y_1)
+    pl.semaphore_wait(barrier, peers)
+    for group in (X_1, Y_1, Z_H, Z_P):
+        start(group)
 
     loads[3].wait()
     for r in range(0, nx, 32):
@@ -241,76 +239,82 @@
         col_send[...] = col[...] + above[...]
         chain(col_send).start()
 
-    def spread_x(src, offset, dst):
-        for side, row in ((0, PAD - 1), (1, PAD + nx)):
-            for z in range(nz):
-                dst[z + 1, pl.ds(row, 1), :] = src[side, pl.ds(offset + z, 1), :]
-
-    arrived(X_1)
-    spread_x(xr, 0, pv)
-    spread_x(xr, nz, hv)
-    arrived(Y_1)
-
-    def first(z, below=True, above_known=False):
+    def first(z, carry):
         for r in range(0, nx, ROWS):
             at = lambda ref, dz, dx: ref[z + 1 + dz, pl.ds(PAD + r + dx, ROWS), :]
             rows = pl.ds(r, ROWS)
             h, p = at(hv, 0, 0), at(pv, 0, 0)
-            h_before, h_after = beside_y(h, *unpacked(yr, nz + z, rows))
-            p_before, p_after = beside_y(p, *unpacked(yr, z, rows))
-            t_zm = tz[z, rows, :] if below else rec(h + at(hv, -1, 0))
-            t_zp = tz[z + 1, rows, :] if above_known else rec(h + at(hv, 1, 0))
+            t_zm, t_zp = tz[z, rows, :], rec(h + at(hv, 1, 0))
             t_xm, t_xp = rec(h + at(hv, 0, -1)), rec(h + at(hv, 0, 1))
-            t_ym, t_yp = rec(h + h_before), rec(h + h_after)
-            diag = 1.0 + ((t_zm + t_zp) + (t_xm + t_xp) + (t_ym + t_yp))
-            inv = rec(diag)
-            total = (p + (t_zm * at(pv, -1, 0) + t_zp * at(pv, 1, 0))
-                     + (t_xm * at(pv, 0, -1) + t_xp * at(pv, 0, 1))
-                     + (t_ym * p_before + t_yp * p_after))
-            if not below:
-                tz[z, rows, :] = t_zm
-            if not above_known:
-                tz[z + 1, rows, :] = t_zp
+            last = lax.broadcasted_iota(jnp.int32, h.shape, 1) == ny - 1
+            t_yp = jnp.where(last, 0.0, rec(h + shifted(h, False)))
+            t_ym = shifted(t_yp, True)
+            tz[z + 1, rows, :] = t_zp
             tx[z, rows, :] = t_xm
             if r + ROWS == nx:
                 tx[z, pl.ds(nx, 1), :] = t_xp[ROWS - 1:, :]
-            tym[z, rows, :] = t_ym
-            typ[z, rows, :] = t_yp
-            rd[z, rows, :] = STEP_RES * inv
-            qv[z + 1, pl.ds(PAD + r, ROWS), :] = total * inv
-
-    first(1, below=False)
-    lax.fori_loop(2, nz // 2, lambda z, c: (first(z), c)[1], 0)
+            ty[z, rows, :] = t_yp
+            rd[z, rows, :] = 1.0 + ((t_zm + t_zp) + (t_xm + t_xp) + (t_ym + t_yp))
+            part[z, rows, :] = (
+                p + (t_zm * at(pv, -1, 0) + t_zp * at(pv, 1, 0))
+                + (t_xm * at(pv, 0, -1) + t_xp * at(pv, 0, 1))
+                + (shifted(t_yp * p, True) + t_yp * shifted(p, False)))
+        return carry
+
+    lax.fori_loop(0, nz // 2, first, 0)
 
     @pl.when(me["slab"] == 1)
     def _():
         forward()
 
-    lax.fori_loop(nz // 2, nz - 1, lambda z, c: (first(z), c)[1], 0)
+    lax.fori_loop(nz // 2, nz, first, 0)
+
+    x_rows = ((0, 0), (1, nx - 1))
+    arrived(X_1)
+    for side, row in x_rows:
+        link = rec(xs[1 - side, pl.ds(nz, nz), :] + xr[side, pl.ds(nz, nz), :])
+        x_link[side] = link
+        flow = link * xr[side, pl.ds(0, nz), :]
+        for z in range(nz):
+            one = pl.ds(row, 1)
+            rd[z, one, :] += link[z:z + 1, :]
+            part[z, one, :] += flow[z:z + 1, :]
+    arrived(Y_1)
+    for side in range(2):
+        link = pltpu.roll(rec(ys[1 - side] + yr[side]), 128 - nz, 1)
+        link = jnp.where(lane_y < nz, link, 0.0)
+        y_link[side] = link
+        y_flow[side] = link * yr[side]
     arrived(Z_H)
     arrived(Z_P)
-    first(0, below=False, above_known=True)
-    first(nz - 1)
+    for side, z in ((0, 0), (1, nz - 1)):
+        for r in range(0, nx, 32):
+            rows = pl.ds(r, 32)
+            link = rec(hv[z + 1, pl.ds(PAD + r, 32), :] + zhr[side, rows, :])
+            z_link[side, rows, :] = link
+            rd[z, rows, :] += link
+            part[z, rows, :] += link * zpr[side, rows, :]
+
+    def divide(z):
+        for r in range(0, nx, 32):
+            rows = pl.ds(r, 32)
+            inv = rec(rd[z, rows, :] + at_edges(y_link, z, rows, ny))
+            rd[z, rows, :] = STEP_RES * inv
+            qv[z + 1, pl.ds(PAD + r, 32), :] = inv * (
+                part[z, rows, :] + at_edges(y_flow, z, rows, ny))
+
+    divide(0)
+    divide(nz - 1)
     start(Z_Q)
+    lax.fori_loop(1, nz - 1, lambda z, c: (divide(z), c)[1], 0)
     face_x(qv, xqs, 0)
     start(X_Q)
     face_y((qv,), yqs)
     start(Y_Q)
 
+    face_y((rd,), edge, 0, 0)
     for side in range(2):
-        for r in range(0, nx, 32):
-            rows, lane = pl.ds(r, 32), lane_y[:32]
-            acc = jnp.zeros((32, 128), jnp.float32)
-            for z in range(nz):
-                if side == 0:
-                    term = tym[z, rows, pl.ds(0, 128)] * rd[z, rows, pl.ds(0, 128)]
-                    moved = pltpu.roll(term, z, 1) if z else term
-                else:
-                    lanes = pl.ds(ny - 128, 128)
-                    term = typ[z, rows, lanes] * rd[z, rows, lanes]
-                    moved = pltpu.roll(term, z + 1, 1)
-                acc = jnp.where(lane == z, moved, acc)
-            edge[side, rows, :] = acc
+        y_link[side] = y_link[side] * edge[1 - side]
 
     @pl.when(me["slab"] == 2)
     def _():
@@ -321,28 +325,29 @@
             at = lambda ref, dz, dx: ref[z + 1 + dz, pl.ds(PAD + r + dx, ROWS), :]
             rows = pl.ds(r, ROWS)
             p, q = at(pv, 0, 0), at(qv, 0, 0)
-            q_before, q_after = beside_y(q, 0.0, 0.0)
+            t_yp = ty[z, rows, :]
             total = (p + (tz[z, rows, :] * at(qv, -1, 0) + tz[z + 1, rows, :] * at(qv, 1, 0))
                      + (tx[z, rows, :] * at(qv, 0, -1) + tx[z, pl.ds(r + 1, ROWS), :] * at(qv, 0, 1))
-                     + (tym[z, rows, :] * q_before + typ[z, rows, :] * q_after))
+                     + (shifted(t_yp * q, True) + t_yp * shifted(q, False)))
             part[z, rows, :] = q + STEP_KEEP * (q - p) + (total * rd[z, rows, :] - STEP_RES * q)
         return carry
 
     lax.fori_loop(0, nz, second, 0)
 
     arrived(X_Q)
-    for side, row in ((0, 0), (1, nx - 1)):
+    for side, row in x_rows:
+        flow = x_link[side] * xqr[side]
         for z in range(nz):
             one = pl.ds(row, 1)
-            part[z, one, :] += rd[z, one, :] * tx[z, pl.ds(row + side, 1), :] * xqr[side, pl.ds(z, 1), :]
+            part[z, one, :] += rd[z, one, :] * flow[z:z + 1, :]
     arrived(Y_Q)
     for side in range(2):
-        y_term[side] = edge[side] * yqr[side]
+        y_term[side] = y_link[side] * yqr[side]
     arrived(Z_Q)
     for side, z in ((0, 0), (1, nz - 1)):
         for r in range(0, nx, 32):
             rows = pl.ds(r, 32)
-            part[z, rows, :] += rd[z, rows, :] * tz[z + side, rows, :] * zqr[side, rows, :]
+            part[z, rows, :] += rd[z, rows, :] * z_link[side, rows, :] * zqr[side, rows, :]
     for z in range(nz):
         solid_wide[z] = jnp.full((8, 128), solid[z], jnp.float32)
 
@@ -361,7 +366,6 @@
 def finish(part, ob, lit, above, y_term, solid_wide, pn_out, phi_out, thick_out, buf, store_sem):
     nz, nx, ny = lit.shape
     outs = (pn_out, phi_out, thick_out)
-    lane = lax.broadcasted_iota(jnp.int32, (ROWS, 128), 1)
 
     def store(i, z):
         return pltpu.make_async_copy(buf.at[i, z], outs[i].at[z], store_sem.at[i, z])
@@ -371,10 +375,7 @@
         solid = jnp.concatenate([solid] * (ROWS // 8), axis=0)
         for r in range(0, nx, ROWS):
             rows = pl.ds(r, ROWS)
-            lo, hi = unpacked(y_term, z, rows)
-            lo, hi = jnp.where(lane == 0, lo, 0.0), jnp.where(lane == 127, hi, 0.0)
-            zeros = [jnp.zeros((ROWS, 128), jnp.float32)] * (ny // 128 - 2)
-            pn = part[z, rows, :] + jnp.concatenate([lo] + zeros + [hi], axis=1)
+            pn = part[z, rows, :] + at_edges(y_term, z, rows, ny)
             stress = jnp.maximum(above[rows, :] + ob[z, rows, :] - pn, 0.0)
             cls = classes(lit[z, rows, :])
             phi = pick(cls, PHI_SURFACE) * jnp.exp2(pick(cls, ATHY_NEG) * stress)
@@ -401,7 +402,7 @@
     shaped = jax.ShapeDtypeStruct
     block, plane = (nz, nx, ny), (nx, ny)
     padded = (nz + 2, nx + 2 * PAD, ny)
-    x_face, y_face = (2, nz, ny), (2, nx, 128)
+    z_face, x_face, y_face = (2, nx, ny), (2, nz, ny), (2, nx, 128)
     vmem = pl.BlockSpec(memory_space=pltpu.VMEM)
     hbm = pl.BlockSpec(memory_space=pltpu.HBM)
     held = (shaped(block, f32), shaped(block, f32), shaped(block, i32), shaped(plane, f32),
@@ -413,9 +414,9 @@
         out_specs=(vmem,) * len(held),
         scratch_shapes=[pltpu.VMEM(shape, f32) for shape in (
             padded, padded, padded, (nz + 1, nx, ny), (nz, nx + PAD, ny),
-            block, block, block, block, plane, plane,
-            (2, 2 * nz, ny), (2, 2 * nz, ny), y_face, y_face,
-            (2, nx, ny), x_face, x_face, y_face, y_face, y_face)] + [
+            block, block, block, plane, plane,
+            (2, 2 * nz, ny), (2, 2 * nz, ny), y_face, y_face, z_face, z_face, z_face,
+            x_face, x_face, y_face, y_face, z_face, x_face, y_face, y_face, y_face)] + [
             pltpu.SMEM((nz,), f32),
             pltpu.SemaphoreType.DMA((4,)),
             pltpu.SemaphoreType.DMA((MESSAGES,)),

time: 15.7 us -> 15.2 us (0.968)
  Pallas kernels: 14.9 us -> 14.4 us
    pallas_call x1, Pallas kernels: 13 us -> 12.5 us  [body(): pl.pallas_call(functools.partial(exchange, sizes), out_shape=held, in_spe...]
where the time goes in v5:
time: 15.2 us; the launch traced here: 15 us
  Pallas kernels  14.4 us (95%)
  between operations  0.64 us (4%)
    pallas_call x1, Pallas kernels, body(): pl.pallas_call(functools.partial(exchange, sizes), out_shape=held, in_spe...  12.5 us
    pallas_call x1, Pallas kernels, body(): pl.pallas_call(finish, out_shape=(shaped(block, f32),) * 3, in_specs=[vme...  1.91 us

profile of v5, /device:TPU:1, one launch (start us, length us, event | category | flops | bytes accessed | tf_op | source)
XLA Modules:
  0.0 15.0 jit_solution(13771765145085546974)
XLA Ops:
  0.6 12.5 %exchange.1 = (f32[8,96,256]{2,1,0:T(8,128)S(1)}, f32[8,96,256]{2,1,0:T(8,128)S(1)}, s32[8,96,256]{2,1,0:T(8,128)S(1)}, f32[96,256]{1,0:T(8,128)S(1)}, f32[2,96,...) custom-call(f32[8,96,256]{2,1,0:T(8,128)} %p_hbm.1, f32[8,96,256]{2,1,0:T(8,128)} %por_hbm.1, s32[8,96,256]{2,1,0:T(8,128)} %lit_hbm.1, ...), custom_call_target="tpu_custom_call" | custom-call | tf_op jit(solution)/shard_map/exchange/pallas_call | solution.py:410
  13.1 1.9 %finish.1 = (f32[8,96,256]{2,1,0:T(8,128)}, f32[8,96,256]{2,1,0:T(8,128)}, f32[8,96,256]{2,1,0:T(8,128)}) custom-call(f32[8,96,256]{2,1,0:T(8,128)S(1)} %get-tuple-element.9.part, f32[8,96,256]{2,1,0:T(8,128)S(1)} %get-tuple-element.10.ob, s32[8,96,256]{2,1,0:T(8,128)S(1)} %get-tuple-element.11.lit, f32[96,256]{1,0:T(8,128)S(1)} %get-tuple-element.12.above, ...), custom_call_target="tpu_custom_call" | custom-call | tf_op jit(solution)/shard_map/finish/pallas_call | solution.py:429

commit v6 on v5

--- a/solution.py
+++ b/solution.py
@@ -33,6 +33,7 @@
 MESH = pl.DeviceIdType.MESH
 PAD = 8
 ROWS = 16
+FOLD = 4
 Z_P, Z_H, X_1, Y_1, Z_Q, X_Q, Y_Q, CHAIN = 0, 2, 4, 6, 8, 10, 12, 14
 MESSAGES = 15
 
@@ -74,7 +75,8 @@
 def exchange(sizes, p_hbm, por_hbm, lit_hbm, solid_hbm,
              part, ob, lit, above, y_term, solid_wide,
              pv, qv, hv, tz, tx, ty, rd, por, col, col_send, xs, xr, ys, yr,
-             zpr, zhr, zqr, xqs, xqr, yqs, yqr, z_link, x_link, y_link, y_flow, edge,
+             zpr, zhr, zqr, xqs, xqr, yqs, yqr, z_link, x_link, x_flow,
+             y_link, y_flow, link_fold, edge,
              solid, load_sem, send_sem, recv_sem):
     nz, nx, ny = por.shape
     axes = ("slab", "mapx", "mapy")
@@ -84,13 +86,14 @@
     peers = sum(jnp.where(f, 1, 0) for flags in (has_lo, has_hi) for f in flags.values())
     inner = pl.ds(PAD, nx)
 
-    loads = [
-        pltpu.make_async_copy(por_hbm, por, load_sem.at[0]),
-        pltpu.make_async_copy(lit_hbm, lit, load_sem.at[1]),
-        pltpu.make_async_copy(p_hbm, pv.at[pl.ds(1, nz), inner, :], load_sem.at[2]),
-        pltpu.make_async_copy(solid_hbm, solid, load_sem.at[3]),
-    ]
-    for c in loads:
+    spans = (pl.ds(0, 1), pl.ds(nz - 1, 1), pl.ds(1, nz - 2))
+    loads = []
+    for i, span in enumerate(spans):
+        loads.append(pltpu.make_async_copy(por_hbm.at[span], por.at[span], load_sem.at[2 * i]))
+        loads.append(pltpu.make_async_copy(lit_hbm.at[span], lit.at[span], load_sem.at[2 * i + 1]))
+    load_p = pltpu.make_async_copy(p_hbm, pv.at[pl.ds(1, nz), inner, :], load_sem.at[6])
+    load_solid = pltpu.make_async_copy(solid_hbm, solid, load_sem.at[7])
+    for c in loads + [load_p, load_solid]:
         c.start()
 
     barrier = pltpu.get_barrier_semaphore()
@@ -141,7 +144,7 @@
             def _():
                 message(k, axis, up, src, dst).wait_send()
 
-    lane_y = lax.broadcasted_iota(jnp.int32, (nx, 128), 1)
+    lane_f = lax.broadcasted_iota(jnp.int32, (nx // FOLD, 128), 1)
 
     for layer in (z_lo, z_hi):
         pv[layer, inner, :] = jnp.zeros((nx, ny), jnp.float32)
@@ -171,11 +174,10 @@
 
         @pl.when(jnp.logical_not(flags["mapy"]))
         def _():
-            yr[side] = jnp.where(lane_y < nz, jnp.float32(0.0), jnp.float32(OUTSIDE))
-            yqr[side] = jnp.zeros((nx, 128), jnp.float32)
-
-    loads[0].wait()
-    loads[1].wait()
+            layer = lax.rem(lane_f, 2 * nz)
+            yr[side] = jnp.where(layer < nz, jnp.float32(0.0), jnp.float32(OUTSIDE))
+            yqr[side] = jnp.zeros(yqr.shape[1:], jnp.float32)
+
 
     def half_inverse(z):
         for r in range(0, nx, 32):
@@ -184,67 +186,57 @@
             hv[z + 1, pl.ds(PAD + r, 32), :] = jnp.exp2(
                 pick(cls, HALF_BASE) + pick(cls, HALF_SLOPE) * por[z, rows, :])
 
-    lax.fori_loop(0, nz, lambda z, c: (half_inverse(z), c)[1], 0)
-    loads[2].wait()
+    for i, z in enumerate((0, nz - 1)):
+        loads[2 * i].wait()
+        loads[2 * i + 1].wait()
+        half_inverse(z)
+    pl.semaphore_wait(barrier, peers)
+    start(Z_H)
+    start(Z_P)
+    loads[4].wait()
+    loads[5].wait()
+    lax.fori_loop(1, nz - 1, lambda z, c: (half_inverse(z), c)[1], 0)
+    load_p.wait()
 
     def face_x(src, dst, offset):
         for side, row in ((0, PAD + nx - 1), (1, PAD)):
             for z in range(nz):
                 dst[side, pl.ds(offset + z, 1), :] = src[z + 1, pl.ds(row, 1), :]
 
+    stride, part_rows = 2 * nz, nx // FOLD
+
     def face_y(srcs, dst, first_z=1, first_row=PAD):
         for side in range(2):
-            for r in range(0, nx, 32):
-                acc = jnp.zeros((32, 128), jnp.float32)
-                lane = lane_y[:32]
-                for i, src in enumerate(srcs):
+            acc = jnp.zeros((part_rows, 128), jnp.float32)
+            for i in range(FOLD):
+                for j, src in enumerate(srcs):
                     for z in range(nz):
-                        k = i * nz + z
+                        k = i * stride + j * nz + z
                         lanes = pl.ds(0 if side else ny - 128, 128)
-                        column = src[z + first_z, pl.ds(first_row + r, 32), lanes]
+                        rows = pl.ds(first_row + i * part_rows, part_rows)
+                        column = src[z + first_z, rows, lanes]
                         shift = k if side else k + 1
                         moved = pltpu.roll(column, shift, 1) if shift else column
-                        acc = jnp.where(lane == k, moved, acc)
-                dst[side, pl.ds(r, 32), :] = acc
+                        acc = jnp.where(lane_f == k, moved, acc)
+            dst[side] = acc
+
+    def unfold(value, dst, side):
+        for i in range(FOLD):
+            moved = pltpu.roll(value, 128 - i * stride, 1) if i else value
+            dst[side, pl.ds(i * part_rows, part_rows), :] = moved
 
     face_x(pv, xs, 0)
     face_x(hv, xs, nz)
+    start(X_1)
     face_y((pv, hv), ys)
-    pl.semaphore_wait(barrier, peers)
-    for group in (X_1, Y_1, Z_H, Z_P):
-        start(group)
-
-    loads[3].wait()
-    for r in range(0, nx, 32):
-        rows = pl.ds(r, 32)
-
-        def add_layer(z, total):
-            cls = classes(lit[z, rows, :])
-            load = (pick(cls, GRAIN_LESS) + WATER_DENSITY * rec(1.0 - por[z, rows, :])) * solid[z]
-            ob[z, rows, :] = total + 0.5 * load
-            return total + load
-
-        col[rows, :] = lax.fori_loop(0, nz, add_layer, jnp.zeros((32, ny), jnp.float32))
-
-    def chain(src):
-        return message(CHAIN, "slab", True, src, above)
-
-    @pl.when(me["slab"] == 0)
-    def _():
-        col_send[...] = col[...]
-        chain(col_send).start()
-
-    def forward():
-        chain(col_send).wait_recv()
-        col_send[...] = col[...] + above[...]
-        chain(col_send).start()
+    start(Y_1)
 
     def first(z, carry):
         for r in range(0, nx, ROWS):
             at = lambda ref, dz, dx: ref[z + 1 + dz, pl.ds(PAD + r + dx, ROWS), :]
             rows = pl.ds(r, ROWS)
             h, p = at(hv, 0, 0), at(pv, 0, 0)
-            t_zm, t_zp = tz[z, rows, :], rec(h + at(hv, 1, 0))
+            t_zm, t_zp = rec(h + at(hv, -1, 0)), rec(h + at(hv, 1, 0))
             t_xm, t_xp = rec(h + at(hv, 0, -1)), rec(h + at(hv, 0, 1))
             last = lax.broadcasted_iota(jnp.int32, h.shape, 1) == ny - 1
             t_yp = jnp.where(last, 0.0, rec(h + shifted(h, False)))
@@ -261,30 +253,64 @@
                 + (shifted(t_yp * p, True) + t_yp * shifted(p, False)))
         return carry
 
-    lax.fori_loop(0, nz // 2, first, 0)
-
-    @pl.when(me["slab"] == 1)
+    first(0, 0)
+    first(nz - 1, 0)
+
+    load_solid.wait()
+    for r in range(0, nx, 32):
+        rows = pl.ds(r, 32)
+
+        def add_layer(z, total):
+            cls = classes(lit[z, rows, :])
+            load = (pick(cls, GRAIN_LESS) + WATER_DENSITY * rec(1.0 - por[z, rows, :])) * solid[z]
+            ob[z, rows, :] = total + 0.5 * load
+            return total + load
+
+        col[rows, :] = lax.fori_loop(0, nz, add_layer, jnp.zeros((32, ny), jnp.float32))
+
+    def chain(src):
+        return message(CHAIN, "slab", True, src, above)
+
+    @pl.when(me["slab"] == 0)
     def _():
-        forward()
-
-    lax.fori_loop(nz // 2, nz, first, 0)
+        col_send[...] = col[...]
+        chain(col_send).start()
+
+    def forward():
+        chain(col_send).wait_recv()
+        col_send[...] = col[...] + above[...]
+        chain(col_send).start()
 
     x_rows = ((0, 0), (1, nx - 1))
     arrived(X_1)
     for side, row in x_rows:
         link = rec(xs[1 - side, pl.ds(nz, nz), :] + xr[side, pl.ds(nz, nz), :])
         x_link[side] = link
-        flow = link * xr[side, pl.ds(0, nz), :]
-        for z in range(nz):
+        x_flow[side] = link * xr[side, pl.ds(0, nz), :]
+
+    def add_x(z):
+        for side, row in x_rows:
             one = pl.ds(row, 1)
-            rd[z, one, :] += link[z:z + 1, :]
-            part[z, one, :] += flow[z:z + 1, :]
+            rd[z, one, :] += x_link[side, pl.ds(z, 1), :]
+            part[z, one, :] += x_flow[side, pl.ds(z, 1), :]
+
     arrived(Y_1)
     for side in range(2):
         link = pltpu.roll(rec(ys[1 - side] + yr[side]), 128 - nz, 1)
-        link = jnp.where(lane_y < nz, link, 0.0)
-        y_link[side] = link
-        y_flow[side] = link * yr[side]
+        link_fold[side] = link
+        unfold(link, y_link, side)
+        unfold(link * yr[side], y_flow, side)
+
+    def divide(z):
+        for r in range(0, nx, 32):
+            rows = pl.ds(r, 32)
+            inv = rec(rd[z, rows, :] + at_edges(y_link, z, rows, ny))
+            rd[z, rows, :] = STEP_RES * inv
+            qv[z + 1, pl.ds(PAD + r, 32), :] = inv * (
+                part[z, rows, :] + at_edges(y_flow, z, rows, ny))
+
+    add_x(0)
+    add_x(nz - 1)
     arrived(Z_H)
     arrived(Z_P)
     for side, z in ((0, 0), (1, nz - 1)):
@@ -294,18 +320,18 @@
             z_link[side, rows, :] = link
             rd[z, rows, :] += link
             part[z, rows, :] += link * zpr[side, rows, :]
-
-    def divide(z):
-        for r in range(0, nx, 32):
-            rows = pl.ds(r, 32)
-            inv = rec(rd[z, rows, :] + at_edges(y_link, z, rows, ny))
-            rd[z, rows, :] = STEP_RES * inv
-            qv[z + 1, pl.ds(PAD + r, 32), :] = inv * (
-                part[z, rows, :] + at_edges(y_flow, z, rows, ny))
-
-    divide(0)
-    divide(nz - 1)
+        divide(z)
     start(Z_Q)
+
+    lax.fori_loop(1, nz // 2, first, 0)
+
+    @pl.when(me["slab"] == 1)
+    def _():
+        forward()
+
+    lax.fori_loop(nz // 2, nz - 1, first, 0)
+    for z in range(1, nz - 1):
+        add_x(z)
     lax.fori_loop(1, nz - 1, lambda z, c: (divide(z), c)[1], 0)
     face_x(qv, xqs, 0)
     start(X_Q)
@@ -314,7 +340,7 @@
 
     face_y((rd,), edge, 0, 0)
     for side in range(2):
-        y_link[side] = y_link[side] * edge[1 - side]
+        link_fold[side] = link_fold[side] * edge[1 - side]
 
     @pl.when(me["slab"] == 2)
     def _():
@@ -342,7 +368,7 @@
             part[z, one, :] += rd[z, one, :] * flow[z:z + 1, :]
     arrived(Y_Q)
     for side in range(2):
-        y_term[side] = y_link[side] * yqr[side]
+        unfold(link_fold[side] * yqr[side], y_term, side)
     arrived(Z_Q)
     for side, z in ((0, 0), (1, nz - 1)):
         for r in range(0, nx, 32):
@@ -402,6 +428,7 @@
     shaped = jax.ShapeDtypeStruct
     block, plane = (nz, nx, ny), (nx, ny)
     padded = (nz + 2, nx + 2 * PAD, ny)
+    folded = (2, nx // FOLD, 128)
     z_face, x_face, y_face = (2, nx, ny), (2, nz, ny), (2, nx, 128)
     vmem = pl.BlockSpec(memory_space=pltpu.VMEM)
     hbm = pl.BlockSpec(memory_space=pltpu.HBM)
@@ -415,10 +442,11 @@
         scratch_shapes=[pltpu.VMEM(shape, f32) for shape in (
             padded, padded, padded, (nz + 1, nx, ny), (nz, nx + PAD, ny),
             block, block, block, plane, plane,
-            (2, 2 * nz, ny), (2, 2 * nz, ny), y_face, y_face, z_face, z_face, z_face,
-            x_face, x_face, y_face, y_face, z_face, x_face, y_face, y_face, y_face)] + [
+            (2, 2 * nz, ny), (2, 2 * nz, ny), folded, folded, z_face, z_face, z_face,
+            x_face, x_face, folded, folded, z_face, x_face, x_face,
+            y_face, y_face, folded, folded)] + [
             pltpu.SMEM((nz,), f32),
-            pltpu.SemaphoreType.DMA((4,)),
+            pltpu.SemaphoreType.DMA((8,)),
             pltpu.SemaphoreType.DMA((MESSAGES,)),
             pltpu.SemaphoreType.DMA((MESSAGES,)),
         ],

time: 15.2 us -> 15.9 us (1.046)
  the two profiles are of different devices: /device:TPU:1 before, /device:TPU:0 now
where the time goes in v6:
time: 15.9 us; the launch traced here: 15.7 us
  Pallas kernels  15.1 us (95%)
  between operations  0.64 us (4%)
    pallas_call x1, Pallas kernels, body(): pl.pallas_call(functools.partial(exchange, sizes), out_shape=held, in_spe...  13.2 us
    pallas_call x1, Pallas kernels, body(): pl.pallas_call(finish, out_shape=(shaped(block, f32),) * 3, in_specs=[vme...  1.91 us

profile of v6, /device:TPU:0, one launch (start us, length us, event | category | flops | bytes accessed | tf_op | source)
XLA Modules:
  0.0 15.7 jit_solution(4959304944869487177)
XLA Ops:
  0.6 13.2 %exchange.1 = (f32[8,96,256]{2,1,0:T(8,128)S(1)}, f32[8,96,256]{2,1,0:T(8,128)S(1)}, s32[8,96,256]{2,1,0:T(8,128)S(1)}, f32[96,256]{1,0:T(8,128)S(1)}, f32[2,96,...) custom-call(f32[8,96,256]{2,1,0:T(8,128)} %p_hbm.1, f32[8,96,256]{2,1,0:T(8,128)} %por_hbm.1, s32[8,96,256]{2,1,0:T(8,128)} %lit_hbm.1, ...), custom_call_target="tpu_custom_call" | custom-call | tf_op jit(solution)/shard_map/exchange/pallas_call | solution.py:437
  13.8 1.9 %finish.1 = (f32[8,96,256]{2,1,0:T(8,128)}, f32[8,96,256]{2,1,0:T(8,128)}, f32[8,96,256]{2,1,0:T(8,128)}) custom-call(f32[8,96,256]{2,1,0:T(8,128)S(1)} %get-tuple-element.9.part, f32[8,96,256]{2,1,0:T(8,128)S(1)} %get-tuple-element.10.ob, s32[8,96,256]{2,1,0:T(8,128)S(1)} %get-tuple-element.11.lit, f32[96,256]{1,0:T(8,128)S(1)} %get-tuple-element.12.above, ...), custom_call_target="tpu_custom_call" | custom-call | tf_op jit(solution)/shard_map/finish/pallas_call | solution.py:457

commit v7 on v6

--- a/solution.py
+++ b/solution.py
@@ -186,16 +186,40 @@
             hv[z + 1, pl.ds(PAD + r, 32), :] = jnp.exp2(
                 pick(cls, HALF_BASE) + pick(cls, HALF_SLOPE) * por[z, rows, :])
 
-    for i, z in enumerate((0, nz - 1)):
-        loads[2 * i].wait()
-        loads[2 * i + 1].wait()
-        half_inverse(z)
+    for load in loads[:4]:
+        load.wait()
+    lax.fori_loop(0, 2, lambda i, c: (half_inverse(i * (nz - 1)), c)[1], 0)
     pl.semaphore_wait(barrier, peers)
     start(Z_H)
     start(Z_P)
     loads[4].wait()
     loads[5].wait()
     lax.fori_loop(1, nz - 1, lambda z, c: (half_inverse(z), c)[1], 0)
+    load_solid.wait()
+    for r in range(0, nx, 32):
+        rows = pl.ds(r, 32)
+
+        def add_layer(z, total):
+            cls = classes(lit[z, rows, :])
+            load = (pick(cls, GRAIN_LESS) + WATER_DENSITY * rec(1.0 - por[z, rows, :])) * solid[z]
+            ob[z, rows, :] = total + 0.5 * load
+            return total + load
+
+        col[rows, :] = lax.fori_loop(0, nz, add_layer, jnp.zeros((32, ny), jnp.float32))
+
+    def chain(src):
+        return message(CHAIN, "slab", True, src, above)
+
+    @pl.when(me["slab"] == 0)
+    def _():
+        col_send[...] = col[...]
+        chain(col_send).start()
+
+    def forward():
+        chain(col_send).wait_recv()
+        col_send[...] = col[...] + above[...]
+        chain(col_send).start()
+
     load_p.wait()
 
     def face_x(src, dst, offset):
@@ -206,19 +230,21 @@
     stride, part_rows = 2 * nz, nx // FOLD
 
     def face_y(srcs, dst, first_z=1, first_row=PAD):
-        for side in range(2):
-            acc = jnp.zeros((part_rows, 128), jnp.float32)
-            for i in range(FOLD):
-                for j, src in enumerate(srcs):
-                    for z in range(nz):
+        def pack(z, faces):
+            faces = list(faces)
+            for side in range(2):
+                lanes = pl.ds(0 if side else ny - 128, 128)
+                for i in range(FOLD):
+                    rows = pl.ds(first_row + i * part_rows, part_rows)
+                    for j, src in enumerate(srcs):
                         k = i * stride + j * nz + z
-                        lanes = pl.ds(0 if side else ny - 128, 128)
-                        rows = pl.ds(first_row + i * part_rows, part_rows)
-                        column = src[z + first_z, rows, lanes]
-                        shift = k if side else k + 1
-                        moved = pltpu.roll(column, shift, 1) if shift else column
-                        acc = jnp.where(lane_f == k, moved, acc)
-            dst[side] = acc
+                        moved = pltpu.roll(src[z + first_z, rows, lanes], k if side else k + 1, 1)
+                        faces[side] = jnp.where(lane_f == k, moved, faces[side])
+            return tuple(faces)
+
+        empty = jnp.zeros((part_rows, 128), jnp.float32)
+        for side, face in enumerate(lax.fori_loop(0, nz, pack, (empty, empty))):
+            dst[side] = face
 
     def unfold(value, dst, side):
         for i in range(FOLD):
@@ -253,33 +279,11 @@
                 + (shifted(t_yp * p, True) + t_yp * shifted(p, False)))
         return carry
 
-    first(0, 0)
-    first(nz - 1, 0)
-
-    load_solid.wait()
-    for r in range(0, nx, 32):
-        rows = pl.ds(r, 32)
-
-        def add_layer(z, total):
-            cls = classes(lit[z, rows, :])
-            load = (pick(cls, GRAIN_LESS) + WATER_DENSITY * rec(1.0 - por[z, rows, :])) * solid[z]
-            ob[z, rows, :] = total + 0.5 * load
-            return total + load
-
-        col[rows, :] = lax.fori_loop(0, nz, add_layer, jnp.zeros((32, ny), jnp.float32))
-
-    def chain(src):
-        return message(CHAIN, "slab", True, src, above)
-
-    @pl.when(me["slab"] == 0)
+    lax.fori_loop(0, nz // 2 + 1, lambda k, c: first(lax.rem(k + nz - 1, nz), c), 0)
+
+    @pl.when(me["slab"] == 1)
     def _():
-        col_send[...] = col[...]
-        chain(col_send).start()
-
-    def forward():
-        chain(col_send).wait_recv()
-        col_send[...] = col[...] + above[...]
-        chain(col_send).start()
+        forward()
 
     x_rows = ((0, 0), (1, nx - 1))
     arrived(X_1)
@@ -320,16 +324,15 @@
             z_link[side, rows, :] = link
             rd[z, rows, :] += link
             part[z, rows, :] += link * zpr[side, rows, :]
-        divide(z)
+    lax.fori_loop(0, 2, lambda i, c: (divide(i * (nz - 1)), c)[1], 0)
     start(Z_Q)
 
-    lax.fori_loop(1, nz // 2, first, 0)
-
-    @pl.when(me["slab"] == 1)
+    lax.fori_loop(nz // 2, nz - 1, first, 0)
+
+    @pl.when(me["slab"] == 2)
     def _():
         forward()
 
-    lax.fori_loop(nz // 2, nz - 1, first, 0)
     for z in range(1, nz - 1):
         add_x(z)
     lax.fori_loop(1, nz - 1, lambda z, c: (divide(z), c)[1], 0)
@@ -341,10 +344,6 @@
     face_y((rd,), edge, 0, 0)
     for side in range(2):
         link_fold[side] = link_fold[side] * edge[1 - side]
-
-    @pl.when(me["slab"] == 2)
-    def _():
-        forward()
 
     def second(z, carry):
         for r in range(0, nx, ROWS):

time: 15.9 us -> 16.4 us (1.031)
  Pallas kernels: 15.1 us -> 15.6 us
    pallas_call x1, Pallas kernels: 13.2 us -> 13.7 us  [body(): pl.pallas_call(functools.partial(exchange, sizes), out_shape=held, in_spe...]
where the time goes in v7:
time: 16.4 us; the launch traced here: 16.2 us
  Pallas kernels  15.6 us (95%)
  between operations  0.64 us (4%)
    pallas_call x1, Pallas kernels, body(): pl.pallas_call(functools.partial(exchange, sizes), out_shape=held, in_spe...  13.7 us
    pallas_call x1, Pallas kernels, body(): pl.pallas_call(finish, out_shape=(shaped(block, f32),) * 3, in_specs=[vme...  1.91 us

profile of v7, /device:TPU:0, one launch (start us, length us, event | category | flops | bytes accessed | tf_op | source)
XLA Modules:
  0.0 16.2 jit_solution(9109171568644517111)
XLA Ops:
  0.6 13.7 %exchange.1 = (f32[8,96,256]{2,1,0:T(8,128)S(1)}, f32[8,96,256]{2,1,0:T(8,128)S(1)}, s32[8,96,256]{2,1,0:T(8,128)S(1)}, f32[96,256]{1,0:T(8,128)S(1)}, f32[2,96,...) custom-call(f32[8,96,256]{2,1,0:T(8,128)} %p_hbm.1, f32[8,96,256]{2,1,0:T(8,128)} %por_hbm.1, s32[8,96,256]{2,1,0:T(8,128)} %lit_hbm.1, ...), custom_call_target="tpu_custom_call" | custom-call | tf_op jit(solution)/shard_map/exchange/pallas_call | solution.py:436
  14.3 1.9 %finish.1 = (f32[8,96,256]{2,1,0:T(8,128)}, f32[8,96,256]{2,1,0:T(8,128)}, f32[8,96,256]{2,1,0:T(8,128)}) custom-call(f32[8,96,256]{2,1,0:T(8,128)S(1)} %get-tuple-element.9.part, f32[8,96,256]{2,1,0:T(8,128)S(1)} %get-tuple-element.10.ob, s32[8,96,256]{2,1,0:T(8,128)S(1)} %get-tuple-element.11.lit, f32[96,256]{1,0:T(8,128)S(1)} %get-tuple-element.12.above, ...), custom_call_target="tpu_custom_call" | custom-call | tf_op jit(solution)/shard_map/finish/pallas_call | solution.py:456

commit v8 on v5

--- a/solution.py
+++ b/solution.py
@@ -33,8 +33,10 @@
 MESH = pl.DeviceIdType.MESH
 PAD = 8
 ROWS = 16
-Z_P, Z_H, X_1, Y_1, Z_Q, X_Q, Y_Q, CHAIN = 0, 2, 4, 6, 8, 10, 12, 14
-MESSAGES = 15
+SPLIT = 4
+X_1, Y_1, X_Q, Y_Q = 0, 2, 4, 6
+Z_P, Z_H, Z_Q, CHAIN = 8, 8 + 2 * SPLIT, 8 + 4 * SPLIT, 8 + 6 * SPLIT
+MESSAGES = CHAIN + SPLIT
 
 
 def rec(x):
@@ -112,13 +114,25 @@
     def pair(k, axis, src_up, dst_up, src_down, dst_down):
         return [(k, axis, True, src_up, dst_up), (k + 1, axis, False, src_down, dst_down)]
 
+    cuts = [pl.ds(i * (nx // SPLIT), nx // SPLIT) for i in range(SPLIT)]
+
+    def layers(k, layer, dst):
+        copies = []
+        for i, rows in enumerate(cuts):
+            copies += pair(k + 2 * i, "slab", layer(nz, rows), dst.at[0, rows, :],
+                           layer(1, rows), dst.at[1, rows, :])
+        return copies
+
+    def padded_layer(ref):
+        return lambda z, rows: ref.at[z, pl.ds(PAD + rows.start, rows.size), :]
+
     z_lo, z_hi = 0, nz + 1
     groups = {
-        Z_P: pair(Z_P, "slab", p_hbm.at[nz - 1], zpr.at[0], p_hbm.at[0], zpr.at[1]),
-        Z_H: pair(Z_H, "slab", hv.at[nz, inner, :], zhr.at[0], hv.at[1, inner, :], zhr.at[1]),
+        Z_P: layers(Z_P, lambda z, rows: p_hbm.at[z - 1, rows, :], zpr),
+        Z_H: layers(Z_H, padded_layer(hv), zhr),
         X_1: pair(X_1, "mapx", xs.at[0], xr.at[0], xs.at[1], xr.at[1]),
         Y_1: pair(Y_1, "mapy", ys.at[0], yr.at[0], ys.at[1], yr.at[1]),
-        Z_Q: pair(Z_Q, "slab", qv.at[nz, inner, :], zqr.at[0], qv.at[1, inner, :], zqr.at[1]),
+        Z_Q: layers(Z_Q, padded_layer(qv), zqr),
         X_Q: pair(X_Q, "mapx", xqs.at[0], xqr.at[0], xqs.at[1], xqr.at[1]),
         Y_Q: pair(Y_Q, "mapy", yqs.at[0], yqr.at[0], yqs.at[1], yqr.at[1]),
     }
@@ -226,18 +240,22 @@
 
         col[rows, :] = lax.fori_loop(0, nz, add_layer, jnp.zeros((32, ny), jnp.float32))
 
-    def chain(src):
-        return message(CHAIN, "slab", True, src, above)
+    def chain():
+        return [message(CHAIN + i, "slab", True, col_send.at[rows, :], above.at[rows, :])
+                for i, rows in enumerate(cuts)]
 
     @pl.when(me["slab"] == 0)
     def _():
         col_send[...] = col[...]
-        chain(col_send).start()
+        for copy in chain():
+            copy.start()
 
     def forward():
-        chain(col_send).wait_recv()
+        for copy in chain():
+            copy.wait_recv()
         col_send[...] = col[...] + above[...]
-        chain(col_send).start()
+        for copy in chain():
+            copy.start()
 
     def first(z, carry):
         for r in range(0, nx, ROWS):
@@ -353,14 +371,16 @@
 
     @pl.when(me["slab"] == 3)
     def _():
-        chain(col_send).wait_recv()
+        for copy in chain():
+            copy.wait_recv()
 
     for group in groups:
         sent(group)
 
     @pl.when(has_hi["slab"])
     def _():
-        chain(col_send).wait_send()
+        for copy in chain():
+            copy.wait_send()
 
 
 def finish(part, ob, lit, above, y_term, solid_wide, pn_out, phi_out, thick_out, buf, store_sem):

time: 15.2 us -> 15.6 us (1.026)
  Pallas kernels: 14.4 us -> 14.9 us
    pallas_call x1, Pallas kernels: 12.5 us -> 12.9 us  [body(): pl.pallas_call(functools.partial(exchange, sizes), out_shape=held, in_spe...]
where the time goes in v8:
time: 15.6 us; the launch traced here: 15.5 us
  Pallas kernels  14.9 us (96%)
  between operations  0.64 us (4%)
    pallas_call x1, Pallas kernels, body(): pl.pallas_call(functools.partial(exchange, sizes), out_shape=held, in_spe...  12.9 us
    pallas_call x1, Pallas kernels, body(): pl.pallas_call(finish, out_shape=(shaped(block, f32),) * 3, in_specs=[vme...  1.91 us

profile of v8, /device:TPU:1, one launch (start us, length us, event | category | flops | bytes accessed | tf_op | source)
XLA Modules:
  0.0 15.5 jit_solution(10459754905644276401)
XLA Ops:
  0.6 12.9 %exchange.1 = (f32[8,96,256]{2,1,0:T(8,128)S(1)}, f32[8,96,256]{2,1,0:T(8,128)S(1)}, s32[8,96,256]{2,1,0:T(8,128)S(1)}, f32[96,256]{1,0:T(8,128)S(1)}, f32[2,96,...) custom-call(f32[8,96,256]{2,1,0:T(8,128)} %p_hbm.1, f32[8,96,256]{2,1,0:T(8,128)} %por_hbm.1, s32[8,96,256]{2,1,0:T(8,128)} %lit_hbm.1, ...), custom_call_target="tpu_custom_call" | custom-call | tf_op jit(solution)/shard_map/exchange/pallas_call | solution.py:430
  13.6 1.9 %finish.1 = (f32[8,96,256]{2,1,0:T(8,128)}, f32[8,96,256]{2,1,0:T(8,128)}, f32[8,96,256]{2,1,0:T(8,128)}) custom-call(f32[8,96,256]{2,1,0:T(8,128)S(1)} %get-tuple-element.9.part, f32[8,96,256]{2,1,0:T(8,128)S(1)} %get-tuple-element.10.ob, s32[8,96,256]{2,1,0:T(8,128)S(1)} %get-tuple-element.11.lit, f32[96,256]{1,0:T(8,128)S(1)} %get-tuple-element.12.above, ...), custom_call_target="tpu_custom_call" | custom-call | tf_op jit(solution)/shard_map/finish/pallas_call | solution.py:449

commit v9 on v5

--- a/solution.py
+++ b/solution.py
@@ -185,6 +185,9 @@
                 pick(cls, HALF_BASE) + pick(cls, HALF_SLOPE) * por[z, rows, :])
 
     lax.fori_loop(0, nz, lambda z, c: (half_inverse(z), c)[1], 0)
+    pl.semaphore_wait(barrier, peers)
+    start(Z_H)
+    start(Z_P)
     loads[2].wait()
 
     def face_x(src, dst, offset):
@@ -210,9 +213,8 @@
     face_x(pv, xs, 0)
     face_x(hv, xs, nz)
     face_y((pv, hv), ys)
-    pl.semaphore_wait(barrier, peers)
-    for group in (X_1, Y_1, Z_H, Z_P):
-        start(group)
+    start(X_1)
+    start(Y_1)
 
     loads[3].wait()
     for r in range(0, nx, 32):

time: 15.2 us -> 15.2 us (level)
  the two profiles are of different devices: /device:TPU:1 before, /device:TPU:0 now
where the time goes in v9:
time: 15.2 us; the launch traced here: 15.1 us
  Pallas kernels  14.4 us (95%)
  between operations  0.64 us (4%)
    pallas_call x1, Pallas kernels, body(): pl.pallas_call(functools.partial(exchange, sizes), out_shape=held, in_spe...  12.5 us
    pallas_call x1, Pallas kernels, body(): pl.pallas_call(finish, out_shape=(shaped(block, f32),) * 3, in_specs=[vme...  1.91 us

profile of v9, /device:TPU:0, one launch (start us, length us, event | category | flops | bytes accessed | tf_op | source)
XLA Modules:
  0.0 15.1 jit_solution(17727402824446865826)
XLA Ops:
  0.6 12.5 %exchange.1 = (f32[8,96,256]{2,1,0:T(8,128)S(1)}, f32[8,96,256]{2,1,0:T(8,128)S(1)}, s32[8,96,256]{2,1,0:T(8,128)S(1)}, f32[96,256]{1,0:T(8,128)S(1)}, f32[2,96,...) custom-call(f32[8,96,256]{2,1,0:T(8,128)} %p_hbm.1, f32[8,96,256]{2,1,0:T(8,128)} %por_hbm.1, s32[8,96,256]{2,1,0:T(8,128)} %lit_hbm.1, ...), custom_call_target="tpu_custom_call" | custom-call | tf_op jit(solution)/shard_map/exchange/pallas_call | solution.py:412
  13.2 1.9 %finish.1 = (f32[8,96,256]{2,1,0:T(8,128)}, f32[8,96,256]{2,1,0:T(8,128)}, f32[8,96,256]{2,1,0:T(8,128)}) custom-call(f32[8,96,256]{2,1,0:T(8,128)S(1)} %get-tuple-element.9.part, f32[8,96,256]{2,1,0:T(8,128)S(1)} %get-tuple-element.10.ob, s32[8,96,256]{2,1,0:T(8,128)S(1)} %get-tuple-element.11.lit, f32[96,256]{1,0:T(8,128)S(1)} %get-tuple-element.12.above, ...), custom_call_target="tpu_custom_call" | custom-call | tf_op jit(solution)/shard_map/finish/pallas_call | solution.py:431

commit v10 on v5

--- a/solution.py
+++ b/solution.py
@@ -285,6 +285,15 @@
         link = jnp.where(lane_y < nz, link, 0.0)
         y_link[side] = link
         y_flow[side] = link * yr[side]
+    def divide(z):
+        for r in range(0, nx, 32):
+            rows = pl.ds(r, 32)
+            inv = rec(rd[z, rows, :] + at_edges(y_link, z, rows, ny))
+            rd[z, rows, :] = STEP_RES * inv
+            qv[z + 1, pl.ds(PAD + r, 32), :] = inv * (
+                part[z, rows, :] + at_edges(y_flow, z, rows, ny))
+
+    lax.fori_loop(1, nz - 1, lambda z, c: (divide(z), c)[1], 0)
     arrived(Z_H)
     arrived(Z_P)
     for side, z in ((0, 0), (1, nz - 1)):
@@ -295,18 +304,9 @@
             rd[z, rows, :] += link
             part[z, rows, :] += link * zpr[side, rows, :]
 
-    def divide(z):
-        for r in range(0, nx, 32):
-            rows = pl.ds(r, 32)
-            inv = rec(rd[z, rows, :] + at_edges(y_link, z, rows, ny))
-            rd[z, rows, :] = STEP_RES * inv
-            qv[z + 1, pl.ds(PAD + r, 32), :] = inv * (
-                part[z, rows, :] + at_edges(y_flow, z, rows, ny))
-
     divide(0)
     divide(nz - 1)
     start(Z_Q)
-    lax.fori_loop(1, nz - 1, lambda z, c: (divide(z), c)[1], 0)
     face_x(qv, xqs, 0)
     start(X_Q)
     face_y((qv,), yqs)

time: 15.2 us -> 15.3 us (level)
  the two profiles are of different devices: /device:TPU:1 before, /device:TPU:0 now
where the time goes in v10:
time: 15.3 us; the launch traced here: 15.2 us
  Pallas kernels  14.5 us (95%)
  between operations  0.64 us (4%)
    pallas_call x1, Pallas kernels, body(): pl.pallas_call(functools.partial(exchange, sizes), out_shape=held, in_spe...  12.6 us
    pallas_call x1, Pallas kernels, body(): pl.pallas_call(finish, out_shape=(shaped(block, f32),) * 3, in_specs=[vme...  1.91 us

profile of v10, /device:TPU:0, one launch (start us, length us, event | category | flops | bytes accessed | tf_op | source)
XLA Modules:
  0.0 15.2 jit_solution(17848109268452709664)
XLA Ops:
  0.6 12.6 %exchange.1 = (f32[8,96,256]{2,1,0:T(8,128)S(1)}, f32[8,96,256]{2,1,0:T(8,128)S(1)}, s32[8,96,256]{2,1,0:T(8,128)S(1)}, f32[96,256]{1,0:T(8,128)S(1)}, f32[2,96,...) custom-call(f32[8,96,256]{2,1,0:T(8,128)} %p_hbm.1, f32[8,96,256]{2,1,0:T(8,128)} %por_hbm.1, s32[8,96,256]{2,1,0:T(8,128)} %lit_hbm.1, ...), custom_call_target="tpu_custom_call" | custom-call | tf_op jit(solution)/shard_map/exchange/pallas_call | solution.py:410
  13.3 1.9 %finish.1 = (f32[8,96,256]{2,1,0:T(8,128)}, f32[8,96,256]{2,1,0:T(8,128)}, f32[8,96,256]{2,1,0:T(8,128)}) custom-call(f32[8,96,256]{2,1,0:T(8,128)S(1)} %get-tuple-element.9.part, f32[8,96,256]{2,1,0:T(8,128)S(1)} %get-tuple-element.10.ob, s32[8,96,256]{2,1,0:T(8,128)S(1)} %get-tuple-element.11.lit, f32[96,256]{1,0:T(8,128)S(1)} %get-tuple-element.12.above, ...), custom_call_target="tpu_custom_call" | custom-call | tf_op jit(solution)/shard_map/finish/pallas_call | solution.py:429
